TPU v7x, 512 devices: a whole 4x4x16 slice. The times are simulated.
512 devices in a mesh: dp: 4 (over x), mx: 16 (over z_hi, y), my: 8 (over z_lo, core).
Axes of the slice: x: 4, y: 4, z: 16 (z_hi: 4, z_lo: 4; z = z_hi * 4 + z_lo), core: 2. Of those that a mesh axis runs over, the one named last changes fastest.
Arguments:
- normed: bfloat16 [2048, 6144], P(('dp', 'mx'), 'my'), may hold values from -6 to 6
- cotangent: bfloat16 [2048, 6144], P(('dp', 'mx'), 'my'), may hold values from -3 to 3
- w_in: bfloat16 [6144, 12288], P('my', 'mx'), may hold values from -0.078125 to 0.078125
- w_out: bfloat16 [12288, 6144], P('mx', 'my'), may hold values from -0.0546875 to 0.0546875
Outputs:
- normed_grad: bfloat16 [2048, 6144], P(('dp', 'mx'), 'my')
- w_in_grad: float32 [6144, 12288], P('my', ('mx', 'dp'))
- w_out_grad: float32 [12288, 6144], P(('mx', 'dp'), 'my')
All inputs are finite; a program needn't handle non-finite values.
Results may differ from a plain program's by a relative error of at most 0.029.
Values may be sent and summed in bfloat16 or wider, within the bound.
A program may use at most 64 MiB of HBM per device.

v0:
```python
import jax
import jax.numpy as jnp
from jax import lax
from jax.sharding import PartitionSpec as P


def activate(preact, upstream):
    cumulative = 0.5 * (1.0 + lax.erf(preact * 0.7071067811865476))
    density = jnp.exp(-0.5 * preact * preact) * 0.3989422804014327
    activation = (preact * cumulative).astype(jnp.bfloat16)
    hidden_grad = (upstream * (cumulative + preact * density)).astype(jnp.bfloat16)
    return (activation, hidden_grad)


def per_device(normed, cotangent, w_in, w_out):
    rows_x, rows_g = (
        lax.all_gather(normed, "mx", axis=0, tiled=True),
        lax.all_gather(cotangent, "mx", axis=0, tiled=True),
    )
    pre_part = jnp.dot(rows_x, w_in, preferred_element_type=jnp.float32)
    up_part = jnp.einsum("td,fd->tf", rows_g, w_out, preferred_element_type=jnp.float32)
    preact, upstream = (
        lax.psum(pre_part.astype(jnp.bfloat16), "my").astype(jnp.float32),
        lax.psum(up_part.astype(jnp.bfloat16), "my").astype(jnp.float32),
    )
    activation, hidden_grad = activate(preact, upstream)
    normed_grad = lax.psum_scatter(
        jnp.einsum("tf,df->td", hidden_grad, w_in, preferred_element_type=jnp.float32).astype(
            jnp.bfloat16
        ),
        "mx",
        scatter_dimension=0,
        tiled=True,
    )
    in_term = jnp.einsum("td,tf->df", rows_x, hidden_grad, preferred_element_type=jnp.float32)
    out_term = jnp.einsum("tf,td->fd", activation, rows_g, preferred_element_type=jnp.float32)
    w_in_grad, w_out_grad = (
        lax.psum_scatter(
            in_term.astype(jnp.bfloat16), "dp", scatter_dimension=1, tiled=True
        ).astype(jnp.float32),
        lax.psum_scatter(
            out_term.astype(jnp.bfloat16), "dp", scatter_dimension=0, tiled=True
        ).astype(jnp.float32),
    )
    return (normed_grad, w_in_grad, w_out_grad)


def solution(mesh):
    return jax.shard_map(
        per_device,
        mesh=mesh,
        in_specs=(P(("dp", "mx"), "my"), P(("dp", "mx"), "my"), P("my", "mx"), P("mx", "my")),
        out_specs=(P(("dp", "mx"), "my"), P("my", ("mx", "dp")), P(("mx", "dp"), "my")),
        check_vma=False,
    )
```

profile of v0, /device:TPU:1, one launch (start us, length us, event | category | flops | bytes accessed | tf_op | source)
XLA Modules:
  0.0 412.3 jit_solution(8331002459713191268)
XLA Ops:
  7.2 0.0 copy-start
  7.2 0.0 all-reduce.3.cloned.1.call-start
  7.2 0.0 copy-start.5
  7.2 62.4 %all_gather.7 = bf16[512,768]{1,0:T(8,128)(2,1)S(1)} all-gather(bf16[32,768]{1,0:T(8,128)(2,1)} %param.4), channel_id=1, replica_groups=mesh['dp'=4,'mx'=16,'my'=8] {'mx'}, dimensions={0}, use_global_device_ids=true | all-gather | bytes 835584 | tf_op jit(solution)/shard_map/all_gather | solution.py:17
  69.6 58.4 %all_gather.6 = bf16[512,768]{1,0:T(8,128)(2,1)S(1)} all-gather(bf16[32,768]{1,0:T(8,128)(2,1)} %param.5), channel_id=1, replica_groups=mesh['dp'=4,'mx'=16,'my'=8] {'mx'}, dimensions={0}, use_global_device_ids=true | all-gather | bytes 835584 | tf_op jit(solution)/shard_map/all_gather | solution.py:18
  128.0 0.0 copy-done.5
  128.0 1.7 convolution_convert_fusion.4
  129.7 0.0 copy-done
  129.7 1.7 convolution_convert_fusion.3
  131.4 0.0 all-reduce.3.cloned.1.call-update
  131.4 0.0 reduce-scatter.8.cloned.1.call-start
  131.5 87.6 %all-reduce.3.cloned.1.call-done = (bf16[512,768]{1,0:T(8,128)(2,1)}, bf16[512,768]{1,0:T(8,128)(2,1)}) async-done(((bf16[512,768]{1,0:T(8,128)(2,1)}, bf16[512,768]{1,0:T(8,128)(2,1)}), (bf16[512,768]{1,0:T(8,128)(2,1)}, bf16[512,768]{1,0:T(8,128)(2,1)})) %all-reduce.3.cloned.1.call-update) | async-done | bytes 1572880 | tf_op jit(solution)/shard_map/psum | solution.py:23
  219.1 0.0 copy-start.2
  219.1 3.1 convolution_convert_fusion
  222.2 0.0 reduce-scatter.8.cloned.1.call-update
  222.2 0.0 reduce-scatter.6.cloned.1.call-start
  222.2 0.0 copy-done.2
  222.3 1.0 copy-done.1
  223.3 0.7 fusion.7
  224.1 0.0 copy-start.3
  224.1 0.9 copy-done.3
  224.9 1.9 fusion.9
  226.8 0.0 reduce-scatter.6.cloned.1.call-update
  226.8 0.0 reduce-scatter.4.cloned.1.call-start
  226.9 1.1 copy-done.4
  227.9 1.7 convolution_convert_fusion.2
  229.6 0.0 reduce-scatter.4.cloned.1.call-update
  229.6 25.1 %reduce-scatter.8.cloned.1.call-done = bf16[192,768]{1,0:T(8,128)(2,1)} async-done(((bf16[768,768]{1,0:T(8,128)(2,1)}), bf16[192,768]{1,0:T(8,128)(2,1)}) %reduce-scatter.8.cloned.1.call-update) | async-done | bytes 294928 | tf_op jit(solution)/shard_map/reduce_scatter | solution.py:41
  254.7 1.8 convert_element_type.47
  256.5 32.6 %reduce-scatter.6.cloned.1.call-done = bf16[768,192]{0,1:T(8,128)(2,1)} async-done(((bf16[768,768]{0,1:T(8,128)(2,1)}), bf16[768,192]{0,1:T(8,128)(2,1)}) %reduce-scatter.6.cloned.1.call-update) | async-done | bytes 294928 | tf_op jit(solution)/shard_map/reduce_scatter | solution.py:38
  289.2 1.8 convert_element_type.44
  291.0 114.8 %reduce-scatter.4.cloned.1.call-done = bf16[32,768]{1,0:T(8,128)(2,1)} async-done(((bf16[512,768]{1,0:T(8,128)(2,1)}), bf16[32,768]{1,0:T(8,128)(2,1)}) %reduce-scatter.4.cloned.1.call-update) | async-done | bytes 49168 | tf_op jit(solution)/shard_map/reduce_scatter | solution.py:27
  (2 shorter events, 0.0 us)
Async XLA Ops:
  7.2 122.6 %copy-start = (bf16[768,768]{1,0:T(8,128)(2,1)S(1)}, bf16[768,768]{1,0:T(8,128)(2,1)}, u32[]{:S(2)}) copy-start(bf16[768,768]{1,0:T(8,128)(2,1)} %param.6) | copy-start | bytes 3538948
  7.2 211.9 %all-reduce.3.cloned.1.call-start = ((), (), s32[]{:S(2)}) async-start(), calls=%async_computation.6 | async-start | bytes 3145728 | tf_op jit(solution)/shard_map/psum | solution.py:23
  7.2 120.8 %copy-start.5 = (bf16[768,768]{1,0:T(8,128)(2,1)S(1)}, bf16[768,768]{1,0:T(8,128)(2,1)}, u32[]{:S(2)}) copy-start(bf16[768,768]{1,0:T(8,128)(2,1)} %param.7) | copy-start | bytes 3538948
  131.4 123.3 %reduce-scatter.8.cloned.1.call-start = ((), (), s32[]{:S(2)}) async-start(), calls=%async_computation.5 | async-start | bytes 1474560 | tf_op jit(solution)/shard_map/reduce_scatter | solution.py:41
  219.1 3.2 copy-start.2
  222.2 1.1 copy-start.1
  222.2 67.0 %reduce-scatter.6.cloned.1.call-start = ((), (), s32[]{:S(2)}) async-start(), calls=%async_computation.4 | async-start | bytes 1474560 | tf_op jit(solution)/shard_map/reduce_scatter | solution.py:38
  224.1 0.9 copy-start.3
  226.8 1.1 copy-start.4
  226.8 179.0 %reduce-scatter.4.cloned.1.call-start = ((), (), s32[]{:S(2)}) async-start(), calls=%async_computation.3 | async-start | bytes 835584 | tf_op jit(solution)/shard_map/reduce_scatter | solution.py:27
Sparse Core Ops, SparseCore 0:
  131.5 87.4 all-reduce.2
  222.3 32.3 reduce-scatter.7
  257.6 31.5 reduce-scatter.5
  293.6 112.1 reduce-scatter.3
where the time goes:
time: 414 us; the launch traced here: 412 us
  waiting for transfers between devices  260 us (63%)
  blocking collectives  121 us (29%)
  between operations  13.8 us (3%)
  matrix products  10 us (2%)
  other arithmetic  4.37 us (1%)
    reduce_scatter x1, waiting for transfers between devices, per_device(): lax.psum_scatter(jnp.einsum('tf,df->td', hidden_grad, w_in, preferred_ele...  115 us
    psum x1, waiting for transfers between devices, per_device(): lax.psum(pre_part.astype(jnp.bfloat16), 'my').astype(jnp.float32)  87.6 us
    all_gather x1, blocking collectives, per_device(): lax.all_gather(normed, 'mx', axis=0, tiled=True)  62.4 us
    all_gather x1, blocking collectives, per_device(): lax.all_gather(cotangent, 'mx', axis=0, tiled=True)  58.4 us
    reduce_scatter x1, waiting for transfers between devices, per_device(): lax.psum_scatter(in_term.astype(jnp.bfloat16), 'dp', scatter_dimension=1,...  32.6 us
    reduce_scatter x1, waiting for transfers between devices, per_device(): lax.psum_scatter(out_term.astype(jnp.bfloat16), 'dp', scatter_dimension=0...  25.1 us
  transfers between devices with their start and end apart: 4, of which 4 were waited for; matrix products, arithmetic and copies ran while one was open for 2% of the time, Pallas kernels for 0%

commit v1 on v0

v1 whole, which is shorter than its diff:
```python
import jax
import jax.numpy as jnp
from jax import lax
from jax.experimental import pallas as pl
from jax.experimental.pallas import tpu as pltpu
from jax.sharding import PartitionSpec as P

MESH = pl.DeviceIdType.MESH
BF16, F32 = jnp.bfloat16, jnp.float32

NC = 6
TOK = 512
ROWS = 32
DM = 768
FH = 768
FC = FH // NC
Q = FC // 4
HALF = DM // 2

S_BWD = 8
S_X2 = 9
S_X3 = 10


def nt(a, b):
    return lax.dot_general(a, b, (((1,), (1,)), ((), ())), preferred_element_type=F32)


def nn(a, b):
    return lax.dot_general(a, b, (((1,), (0,)), ((), ())), preferred_element_type=F32)


def tn(a, b):
    return lax.dot_general(a, b, (((0,), (0,)), ((), ())), preferred_element_type=F32)


def activate(preact, upstream):
    cumulative = 0.5 * (1.0 + lax.erf(preact * 0.7071067811865476))
    density = jnp.exp(-0.5 * preact * preact) * 0.3989422804014327
    activation = (preact * cumulative).astype(BF16)
    hidden_grad = (upstream * (cumulative + preact * density)).astype(BF16)
    return activation, hidden_grad


def kernel(
    normed, cotangent, w_in, w_out,
    ng_out, win_out, wout_out,
    xg, win_v, w1t, wo, pu, crecv, zrecv, ah, dw, xr1, xr2, ng, ngb, yr1, yr2, zs, gz1, gz2,
    lsem, az_s, az_r, azf_s, azf_r, ay_s, ay_r, ayf_s, ayf_r,
    co_s, co_r, ch_s, ch_r, bc_s, bc_r, ce_s, ce_r, x1_s, x1_r, x2_s, x2_r,
    gy1_s, gy1_r, gy2_s, gy2_r, gz1_s, gz1_r, gz2_s, gz2_r,
):
    x = lax.axis_index("dp")
    mx = lax.axis_index("mx")
    my = lax.axis_index("my")
    zh, y = mx // 4, mx % 4
    zl, c = my // 2, my % 2
    o = 1 - c

    def at_x(k):
        return {"dp": (x + k) % 4}

    def at_y(k):
        return {"mx": zh * 4 + (y + k) % 4}

    def at_zh(k):
        return {"mx": ((zh + k) % 4) * 4 + y}

    def at_zl(k):
        return {"my": ((zl + k) % 4) * 2 + c}

    at_core = {"my": zl * 2 + o}

    def rc(src, dst, send, recv, device):
        return pltpu.make_async_remote_copy(
            src_ref=src, dst_ref=dst, send_sem=send, recv_sem=recv, device_id=device, device_id_type=MESH
        )

    load_in = pltpu.make_async_copy(w_in, win_v, lsem.at[4])
    load_in.start()
    load_out = [pltpu.make_async_copy(w_out.at[g], wo.at[:, g], lsem.at[g]) for g in range(4)]
    for copy in load_out:
        copy.start()

    barrier = pltpu.get_barrier_semaphore()
    partners = [at_core]
    for k in (1, 3):
        partners += [at_x(k), at_y(k), at_zh(k), at_zl(k)]
    for device in partners:
        pl.semaphore_signal(barrier, inc=1, device_id=device, device_id_type=MESH)
    pl.semaphore_wait(barrier, len(partners))

    STEP = (1, 3)

    def block(k, yy):
        return pl.ds(pl.multiple_of((((zh + k) % 4) * 4 + yy) * ROWS, ROWS), ROWS)

    def own(a):
        return (normed, cotangent)[a]

    def az(d, a):
        return rc(own(a), xg.at[a, block(0, y)], az_s.at[d, a], az_r.at[d, a], at_zh(STEP[d]))

    def az_wait(d, a):
        here = xg.at[a, block(STEP[1 - d], y)]
        rc(here, here, az_s.at[d, a], az_r.at[d, a], at_zh(STEP[d])).wait_recv()

    def azf(d):
        here = xg.at[d, block(STEP[1 - d], y)]
        return rc(here, here, azf_s.at[d], azf_r.at[d], at_zh(STEP[d]))

    def azf_wait(d):
        here = xg.at[d, block(2, y)]
        rc(here, here, azf_s.at[d], azf_r.at[d], at_zh(STEP[d])).wait_recv()

    def ay(k, d, a):
        src = own(a) if k == 0 else xg.at[a, block(k, y)]
        return rc(src, xg.at[a, block(k, y)], ay_s.at[k, d, a], ay_r.at[k, d, a], at_y(STEP[d]))

    def ay_wait(k, d, a):
        here = xg.at[a, block(k, (y + STEP[1 - d]) % 4)]
        rc(here, here, ay_s.at[k, d, a], ay_r.at[k, d, a], at_y(STEP[d])).wait_recv()

    def ayf(k, d):
        here = xg.at[d, block(k, (y + STEP[1 - d]) % 4)]
        return rc(here, here, ayf_s.at[k, d], ayf_r.at[k, d], at_y(STEP[d]))

    def ayf_wait(k, d):
        here = xg.at[d, block(k, (y + 2) % 4)]
        rc(here, here, ayf_s.at[k, d], ayf_r.at[k, d], at_y(STEP[d])).wait_recv()

    for a in range(2):
        az(0, a).start()
        az(1, 1 - a).start()
        ay(0, 0, a).start()
        ay(0, 1, 1 - a).start()
    for a in range(2):
        xg[a, block(0, y)] = own(a)[...]

    load_in.wait()
    for k in range(FH // 128):
        turned = win_v[:, k * 128:(k + 1) * 128].T
        for part in range(128 // Q):
            g, rest = divmod(k * 128 + part * Q, FH // 4)
            w1t[rest // Q, g] = turned[part * Q:(part + 1) * Q]
    for copy in load_out:
        copy.wait()

    for d in range(2):
        ay_wait(0, d, d)
        ayf(0, d).start()
    for d in range(2):
        az_wait(d, d)
        azf(d).start()
        for e in range(2):
            ay(STEP[1 - d], e, d).start()
    for d in range(2):
        az_wait(d, 1 - d)
        for e in range(2):
            ay(STEP[1 - d], e, 1 - d).start()
    for k in (3, 1):
        for d in range(2):
            ay_wait(k, d, d)
            ayf(k, d).start()
    for d in range(2):
        azf_wait(d)
        for e in range(2):
            ay(2, e, d).start()
    for d in range(2):
        ay_wait(2, d, d)
        ayf(2, d).start()
    for k in (0, 3, 1, 2):
        for d in range(2):
            ay_wait(k, d, 1 - d)
            ayf_wait(k, d)

    OWNER = (0, 3)
    TO_OWNER = (3, 1)
    ng[...] = jnp.zeros_like(ng)

    def core_copy(j):
        return rc(pu.at[j, o], crecv.at[j], co_s.at[j], co_r.at[j], at_core)

    def chain(j, side):
        return rc(pu.at[j, c, side], zrecv.at[j, side], ch_s.at[j, side], ch_r.at[j, side], at_zl(TO_OWNER[side]))

    def spread(j, side):
        here = ah.at[j, :, 2 * c + side]
        return rc(here, here, bc_s.at[j, side], bc_r.at[j, side], at_zl(TO_OWNER[1 - side]))

    def core_share(j, side):
        here = ah.at[j, :, 2 * c + side]
        return rc(here, here, ce_s.at[j, side], ce_r.at[j, side], at_core)

    def core_share_wait(j, side):
        here = ah.at[j, :, 2 * o + side]
        rc(here, here, ce_s.at[j, side], ce_r.at[j, side], at_core).wait_recv()

    def x1(j, d):
        return rc(dw.at[j, d, (x + 2) % 4], xr1.at[j, d], x1_s.at[j, d], x1_r.at[j, d], at_x(STEP[d]))

    def x2(j, d):
        return rc(dw.at[j, :, (x + STEP[d]) % 4], xr2.at[j, d], x2_s.at[j, d], x2_r.at[j, d], at_x(STEP[d]))

    def forward(j):
        for a, w in enumerate((w1t, wo)):
            part = nt(w[j].reshape(FC, DM), xg[a]).astype(BF16)
            for q in range(4):
                pu[j, q // 2, q % 2, a] = part[q * Q:(q + 1) * Q]
        core_copy(j).start()

    def add_core(j):
        core_copy(j).wait_recv()
        pu[j, c] = (pu[j, c].astype(F32) + crecv[j].astype(F32)).astype(BF16)
        for side in range(2):
            @pl.when(zl == OWNER[1 - side])
            def _():
                chain(j, side).start()

    def pass_on(j, side):
        chain(j, side).wait_recv()
        pu[j, c, side] = (pu[j, c, side].astype(F32) + zrecv[j, side].astype(F32)).astype(BF16)
        chain(j, side).start()

    def finish(j, side):
        chain(j, side).wait_recv()
        total = [pu[j, c, side, a].astype(F32) + zrecv[j, side, a].astype(F32) for a in range(2)]
        activation, hidden_grad = activate(*total)
        ah[j, 0, 2 * c + side] = activation
        ah[j, 1, 2 * c + side] = hidden_grad
        spread(j, side).start()
        core_share(j, side).start()

    def pass_back(j, side, last):
        spread(j, side).wait_recv()
        if not last:
            spread(j, side).start()
        core_share(j, side).start()

    def backward(j):
        for side in range(2):
            core_share_wait(j, side)
        hidden_grad = ah[j, 1].reshape(FC, TOK)
        dw[j, 0] = nn(hidden_grad, xg[0]).astype(BF16).reshape(4, Q, DM)
        x1(j, 0).start()
        dw[j, 1] = nn(ah[j, 0].reshape(FC, TOK), xg[1]).astype(BF16).reshape(4, Q, DM)
        x1(j, 1).start()
        ng[...] += tn(hidden_grad, w1t[j].reshape(FC, DM))

    def x_step2(j):
        for d in range(2):
            x1(j, d).wait_recv()
            to = (x + STEP[d]) % 4
            dw[j, d, to] = (dw[j, d, to].astype(F32) + xr1[j, d].astype(F32)).astype(BF16)
            x2(j, d).start()

    def x_step3(j):
        for d in range(2):
            x2(j, d).wait_recv()
        rows = pl.ds(pl.multiple_of(j * Q, Q), Q)
        for a, out in enumerate((win_out, wout_out)):
            out[rows] = dw[j, a, x].astype(F32) + xr2[j, 0, a].astype(F32) + xr2[j, 1, a].astype(F32)

    def step(tau, carry):
        def stage(s, run, on=None):
            j = tau - s
            here = (j >= 0) & (j < NC)
            if on is not None:
                here = here & (zl == on)

            @pl.when(here)
            def _():
                run(j)

        for side in range(2):
            at = (lambda i: i) if side == 0 else (lambda i: 3 - i)
            stage(7, lambda j: pass_back(j, side, True), at(3))
            stage(6, lambda j: pass_back(j, side, False), at(2))
            stage(5, lambda j: pass_back(j, side, False), at(1))
            stage(4, lambda j: finish(j, side), at(0))
            stage(3, lambda j: pass_on(j, side), at(1))
            stage(2, lambda j: pass_on(j, side), at(2))
        stage(1, add_core)
        stage(0, forward)
        stage(S_BWD, backward)
        stage(S_X2, x_step2)
        stage(S_X3, x_step3)
        return carry

    lax.fori_loop(0, NC + S_BWD, step, 0)

    for h in range(2):
        ngb[:, :, h] = ng[:, h * HALF:(h + 1) * HALF].astype(BF16).reshape(4, 4, ROWS, HALF)

    def y1(k, d):
        return rc(ngb.at[(zh + k) % 4, (y + 2) % 4, d], yr1.at[k, d], gy1_s.at[k, d], gy1_r.at[k, d], at_y(STEP[d]))

    def y2(k, d):
        to = ngb.at[(zh + k) % 4, (y + STEP[d]) % 4]
        return rc(to, yr2.at[k, d], gy2_s.at[k, d], gy2_r.at[k, d], at_y(STEP[d]))

    def z1(d):
        return rc(zs.at[2, d], gz1.at[d], gz1_s.at[d], gz1_r.at[d], at_zh(STEP[d]))

    def z2(d):
        return rc(zs.at[STEP[d]], gz2.at[d], gz2_s.at[d], gz2_r.at[d], at_zh(STEP[d]))

    order = (2, 1, 3, 0)
    for k in order:
        for d in range(2):
            y1(k, d).start()
    x_step2(NC - 1)
    for k in order:
        for d in range(2):
            y1(k, d).wait_recv()
            zz, to = (zh + k) % 4, (y + STEP[d]) % 4
            ngb[zz, to, d] = (ngb[zz, to, d].astype(F32) + yr1[k, d].astype(F32)).astype(BF16)
            y2(k, d).start()
    x_step3(NC - 2)
    for k in order:
        for d in range(2):
            y2(k, d).wait_recv()
        total = ngb[(zh + k) % 4, y].astype(F32) + yr2[k, 0].astype(F32) + yr2[k, 1].astype(F32)
        zs[k] = total.astype(BF16)
        if k == 2:
            for d in range(2):
                z1(d).start()
    for d in range(2):
        z1(d).wait_recv()
        k = STEP[d]
        zs[k, d] = (zs[k, d].astype(F32) + gz1[d].astype(F32)).astype(BF16)
        z2(d).start()
    x_step3(NC - 1)
    for d in range(2):
        z2(d).wait_recv()
    total = zs[0].astype(F32) + gz2[0].astype(F32) + gz2[1].astype(F32)
    for h in range(2):
        ng_out[:, h * HALF:(h + 1) * HALF] = total[h].astype(BF16)

    for d in range(2):
        for a in range(2):
            az(d, a).wait_send()
        azf(d).wait_send()
        for k in range(4):
            for a in range(2):
                ay(k, d, a).wait_send()
            ayf(k, d).wait_send()
            y1(k, d).wait_send()
            y2(k, d).wait_send()
        z1(d).wait_send()
        z2(d).wait_send()

    def sent(j, carry):
        core_copy(j).wait_send()
        for side in range(2):
            @pl.when(zl != OWNER[side])
            def _():
                chain(j, side).wait_send()

            @pl.when(zl != OWNER[1 - side])
            def _():
                spread(j, side).wait_send()

            core_share(j, side).wait_send()
            x1(j, side).wait_send()
            x2(j, side).wait_send()
        return carry

    lax.fori_loop(0, NC, sent, 0)


def per_device(normed, cotangent, w_in, w_out):
    vmem = pl.BlockSpec(memory_space=pltpu.VMEM)
    anywhere = pl.BlockSpec(memory_space=pl.ANY)
    two = lambda *shape: [pltpu.SemaphoreType.DMA(shape)] * 2
    ng, win_t, wout = pl.pallas_call(
        kernel,
        out_shape=(
            jax.ShapeDtypeStruct((ROWS, DM), BF16),
            jax.ShapeDtypeStruct((FH // 4, DM), F32),
            jax.ShapeDtypeStruct((FH // 4, DM), F32),
        ),
        in_specs=[vmem, vmem, anywhere, anywhere],
        out_specs=[vmem, vmem, vmem],
        scratch_shapes=[
            pltpu.VMEM((2, TOK, DM), BF16),
            pltpu.VMEM((DM, FH), BF16),
            pltpu.VMEM((NC, 4, Q, DM), BF16),
            pltpu.VMEM((NC, 4, Q, DM), BF16),
            pltpu.VMEM((NC, 2, 2, 2, Q, TOK), BF16),
            pltpu.VMEM((NC, 2, 2, Q, TOK), BF16),
            pltpu.VMEM((NC, 2, 2, Q, TOK), BF16),
            pltpu.VMEM((NC, 2, 4, Q, TOK), BF16),
            pltpu.VMEM((NC, 2, 4, Q, DM), BF16),
            pltpu.VMEM((NC, 2, Q, DM), BF16),
            pltpu.VMEM((NC, 2, 2, Q, DM), BF16),
            pltpu.VMEM((TOK, DM), F32),
            pltpu.VMEM((4, 4, 2, ROWS, HALF), BF16),
            pltpu.VMEM((4, 2, ROWS, HALF), BF16),
            pltpu.VMEM((4, 2, 2, ROWS, HALF), BF16),
            pltpu.VMEM((4, 2, ROWS, HALF), BF16),
            pltpu.VMEM((2, ROWS, HALF), BF16),
            pltpu.VMEM((2, 2, ROWS, HALF), BF16),
            pltpu.SemaphoreType.DMA((5,)),
            *two(2, 2), *two(2), *two(4, 2, 2), *two(4, 2),
            *two(NC), *two(NC, 2), *two(NC, 2), *two(NC, 2), *two(NC, 2), *two(NC, 2),
            *two(4, 2), *two(4, 2), *two(2), *two(2),
        ],
        compiler_params=pltpu.CompilerParams(
            collective_id=0, has_side_effects=True, vmem_limit_bytes=48 * 1024 * 1024
        ),
        name="mlp_branch",
    )(normed, cotangent, w_in, w_out.reshape(4, NC, Q, DM))
    return ng, win_t.T, wout


def solution(mesh):
    return jax.shard_map(
        per_device,
        mesh=mesh,
        in_specs=(P(("dp", "mx"), "my"), P(("dp", "mx"), "my"), P("my", "mx"), P("mx", "my")),
        out_specs=(P(("dp", "mx"), "my"), P("my", ("mx", "dp")), P(("mx", "dp"), "my")),
        check_vma=False,
    )
```

time: 414 us -> 118 us (0.29)
  the two profiles are of different devices: /device:TPU:1 before, /device:TPU:8 now
where the time goes in v1:
time: 118 us
  Pallas kernels  111 us (94%)
  local copies, waits for them, and re-layouts  6.38 us (5%)
    pallas_call x1, Pallas kernels, per_device(): pl.pallas_call(kernel, out_shape=(jax.ShapeDtypeStruct((ROWS, DM), BF16),...  111 us
    unnamed x11, local copies, waits for them, and re-layouts  6.38 us

profile of v1, /device:TPU:8, one launch (start us, length us, event | category | flops | bytes accessed | tf_op | source)
XLA Modules:
  0.0 117.8 jit_solution(3512534296814546310)
XLA Ops:
  0.6 0.0 copy-start
  0.6 1.3 %copy-done = bf16[768,768]{1,0:T(8,128)(2,1)S(1)} copy-done((bf16[768,768]{1,0:T(8,128)(2,1)S(1)}, bf16[768,768]{1,0:T(8,128)(2,1)}, u32[]{:S(2)}) %copy-start) | copy-done | bytes 1179672
  1.9 0.0 copy-start.1
  1.9 1.3 %copy-done.1 = bf16[768,768]{1,0:T(8,128)(2,1)S(1)} copy-done((bf16[768,768]{1,0:T(8,128)(2,1)S(1)}, bf16[768,768]{1,0:T(8,128)(2,1)}, u32[]{:S(2)}) %copy-start.1) | copy-done | bytes 1179672
  3.2 0.0 copy-start.2
  3.2 0.8 copy-done.2
  4.0 0.0 copy-start.3
  4.0 0.8 copy-done.3
  4.8 110.7 %mlp_branch.1 = (bf16[32,768]{1,0:T(8,128)(2,1)S(1)}, f32[192,768]{1,0:T(8,128)S(1)}, f32[192,768]{1,0:T(8,128)S(1)}) custom-call(bf16[32,768]{1,0:T(8,128)(2,1)S(1)} %copy-done.2, bf16[32,768]{1,0:T(8,128)(2,1)S(1)} %copy-done.3, bf16[768,768]{1,0:T(8,128)(2,1)S(1)} %copy-done, bf16[4,6,32,768]{3,2,1,0:T(8,128)(2,1)S(1)} %bitcast.2), custom_call_target="tpu_custom_call" | custom-call | tf_op jit(solution)/shard_map/mlp_branch/pallas_call | solution.py:376
  115.5 0.6 copy.10
  116.1 0.8 copy.11
  116.9 0.8 copy.12
Async XLA Ops:
  0.6 1.3 %copy-start = (bf16[768,768]{1,0:T(8,128)(2,1)S(1)}, bf16[768,768]{1,0:T(8,128)(2,1)}, u32[]{:S(2)}) copy-start(bf16[768,768]{1,0:T(8,128)(2,1)} %w_in.1) | copy-start | bytes 3538948
  1.9 1.3 %copy-start.1 = (bf16[768,768]{1,0:T(8,128)(2,1)S(1)}, bf16[768,768]{1,0:T(8,128)(2,1)}, u32[]{:S(2)}) copy-start(bf16[768,768]{1,0:T(8,128)(2,1)} %param.7) | copy-start | bytes 3538948
  3.2 0.8 copy-start.2
  4.0 0.8 copy-start.3

commit v2 on v1

v2 whole, which is shorter than its diff:
```python
import jax
import jax.numpy as jnp
from jax import lax
from jax.experimental import pallas as pl
from jax.experimental.pallas import tpu as pltpu
from jax.sharding import PartitionSpec as P

MESH = pl.DeviceIdType.MESH
BF16, F32 = jnp.bfloat16, jnp.float32

NC = 6
TOK = 512
ROWS = 32
PIECE = ROWS // 2
DM = 768
FH = 768
FC = FH // NC
Q = FC // 4
HALF = DM // 2

S_BWD = 5
S_X2 = 6
S_X3 = 7


def nt(a, b):
    return lax.dot_general(a, b, (((1,), (1,)), ((), ())), preferred_element_type=F32)


def nn(a, b):
    return lax.dot_general(a, b, (((1,), (0,)), ((), ())), preferred_element_type=F32)


def tn(a, b):
    return lax.dot_general(a, b, (((0,), (0,)), ((), ())), preferred_element_type=F32)


def activate(preact, upstream):
    cumulative = 0.5 * (1.0 + lax.erf(preact * 0.7071067811865476))
    density = jnp.exp(-0.5 * preact * preact) * 0.3989422804014327
    activation = (preact * cumulative).astype(BF16)
    hidden_grad = (upstream * (cumulative + preact * density)).astype(BF16)
    return activation, hidden_grad


def kernel(
    normed, cotangent, w_in, w_out,
    ng_out, win_out, wout_out,
    xg, win_v, w1t, wo, pu, crecv, zrecv, ah, dw, xr1, xr2, ng, ngb, yr1, yr2, zs, gz1, gz2,
    lsem, az_s, az_r, azf_s, azf_r, ay_s, ay_r, ayf_s, ayf_r,
    co_s, co_r, ne_s, ne_r, ch_s, ch_r, sn_s, sn_r, sp_s, sp_r, ce_s, ce_r, x1_s, x1_r, x2_s, x2_r,
    gy1_s, gy1_r, gy2_s, gy2_r, gz1_s, gz1_r, gz2_s, gz2_r,
):
    x = lax.axis_index("dp")
    mx = lax.axis_index("mx")
    my = lax.axis_index("my")
    zh, y = mx // 4, mx % 4
    zl, c = my // 2, my % 2
    o = 1 - c

    def at_x(k):
        return {"dp": (x + k) % 4}

    def at_y(k):
        return {"mx": zh * 4 + (y + k) % 4}

    def at_zh(k):
        return {"mx": ((zh + k) % 4) * 4 + y}

    def at_zl(k):
        return {"my": ((zl + k) % 4) * 2 + c}

    at_core = {"my": zl * 2 + o}

    def rc(src, dst, send, recv, device):
        return pltpu.make_async_remote_copy(
            src_ref=src, dst_ref=dst, send_sem=send, recv_sem=recv, device_id=device, device_id_type=MESH
        )

    STEP = (1, 3)

    def block(k, yy):
        return pl.ds(pl.multiple_of((((zh + k) % 4) * 4 + yy) * ROWS, ROWS), ROWS)

    def part(k, yy, r):
        return pl.ds(pl.multiple_of((((zh + k) % 4) * 4 + yy) * ROWS + r * PIECE, PIECE), PIECE)

    load_own = [pltpu.make_async_copy(t, xg.at[a, block(0, y)], lsem.at[5 + a]) for a, t in enumerate((normed, cotangent))]
    load_in = pltpu.make_async_copy(w_in, win_v, lsem.at[4])
    load_out = [pltpu.make_async_copy(w_out.at[g], wo.at[:, g], lsem.at[g]) for g in range(4)]
    for copy in (*load_own, load_in, *load_out):
        copy.start()

    barrier = pltpu.get_barrier_semaphore()
    partners = [at_core]
    for k in (1, 3):
        partners += [at_x(k), at_y(k), at_zh(k), at_zl(k)]
    for device in partners:
        pl.semaphore_signal(barrier, inc=1, device_id=device, device_id_type=MESH)
    pl.semaphore_wait(barrier, len(partners))

    def az(d, a, r):
        here = xg.at[a, part(0, y, r)]
        return rc(here, here, az_s.at[d, a, r], az_r.at[d, a, r], at_zh(STEP[d]))

    def az_wait(d, a, r):
        here = xg.at[a, part(STEP[1 - d], y, r)]
        rc(here, here, az_s.at[d, a, r], az_r.at[d, a, r], at_zh(STEP[d])).wait_recv()

    def azf(d, r):
        here = xg.at[d, part(STEP[1 - d], y, r)]
        return rc(here, here, azf_s.at[d, r], azf_r.at[d, r], at_zh(STEP[d]))

    def azf_wait(d, r):
        here = xg.at[d, part(2, y, r)]
        rc(here, here, azf_s.at[d, r], azf_r.at[d, r], at_zh(STEP[d])).wait_recv()

    def ay(k, d, a, r):
        here = xg.at[a, part(k, y, r)]
        return rc(here, here, ay_s.at[k, d, a, r], ay_r.at[k, d, a, r], at_y(STEP[d]))

    def ay_wait(k, d, a, r):
        here = xg.at[a, part(k, (y + STEP[1 - d]) % 4, r)]
        rc(here, here, ay_s.at[k, d, a, r], ay_r.at[k, d, a, r], at_y(STEP[d])).wait_recv()

    def ayf(k, d, r):
        here = xg.at[d, part(k, (y + STEP[1 - d]) % 4, r)]
        return rc(here, here, ayf_s.at[k, d, r], ayf_r.at[k, d, r], at_y(STEP[d]))

    def ayf_wait(k, d, r):
        here = xg.at[d, part(k, (y + 2) % 4, r)]
        rc(here, here, ayf_s.at[k, d, r], ayf_r.at[k, d, r], at_y(STEP[d])).wait_recv()

    for copy in load_own:
        copy.wait()
    for a in range(2):
        for r in range(2):
            az(0, a, r).start()
            az(1, 1 - a, r).start()
            ay(0, 0, a, r).start()
            ay(0, 1, 1 - a, r).start()

    load_in.wait()
    for k in range(FH // 128):
        turned = win_v[:, k * 128:(k + 1) * 128].T
        for u in range(128 // Q):
            g, rest = divmod(k * 128 + u * Q, FH // 4)
            w1t[rest // Q, g] = turned[u * Q:(u + 1) * Q]
    for copy in load_out:
        copy.wait()

    def along_y(k, a, r):
        for d in range(2):
            ay(k, d, a, r).start()

    def further_y(k, a, r):
        ay_wait(k, a, a, r)
        ayf(k, a, r).start()

    for r in range(2):
        for a in range(2):
            further_y(0, a, r)
    arrived = [[(0, 0, r), (1, 1, r)] for r in range(2)] + [[(0, 1, r), (1, 0, r)] for r in range(2)]
    previous = None
    for n, pieces in enumerate(arrived):
        for d, a, r in pieces:
            az_wait(d, a, r)
            if d == a:
                azf(d, r).start()
            along_y(STEP[1 - d], a, r)
        if previous is not None:
            for d, a, r in previous:
                further_y(STEP[1 - d], a, r)
        previous = pieces
    for r in range(2):
        for d in range(2):
            azf_wait(d, r)
            along_y(2, d, r)
        for d, a, rr in previous:
            further_y(2 if r else STEP[1 - d], a, rr)
        previous = [(d, d, r) for d in range(2)]
    for d, a, r in previous:
        further_y(2, a, r)
    for k in (0, 3, 1, 2):
        for d in range(2):
            for r in range(2):
                ay_wait(k, d, 1 - d, r)
                ayf_wait(k, d, r)

    NEAR, OWNER, RELAY, FAR = range(4)
    ng[...] = jnp.zeros_like(ng)

    def core_copy(j):
        return rc(pu.at[j, o], crecv.at[j], co_s.at[j], co_r.at[j], at_core)

    def near(j, side, a):
        return rc(
            pu.at[j, c, side, a], zrecv.at[j, side, 0, a], ne_s.at[j, side, a], ne_r.at[j, side, a], at_zl(STEP[side])
        )

    def chain(j, side, a):
        return rc(
            pu.at[j, c, side, a], zrecv.at[j, side, 1, a], ch_s.at[j, side, a], ch_r.at[j, side, a], at_zl(STEP[1 - side])
        )

    def spread_near(j, side, a):
        here = ah.at[j, a, 2 * c + side]
        return rc(here, here, sn_s.at[j, side, a], sn_r.at[j, side, a], at_zl(STEP[1 - side]))

    def spread(j, side, a):
        here = ah.at[j, a, 2 * c + side]
        return rc(here, here, sp_s.at[j, side, a], sp_r.at[j, side, a], at_zl(STEP[side]))

    def core_share(j, side):
        here = ah.at[j, :, 2 * c + side]
        return rc(here, here, ce_s.at[j, side], ce_r.at[j, side], at_core)

    def core_share_wait(j, side):
        here = ah.at[j, :, 2 * o + side]
        rc(here, here, ce_s.at[j, side], ce_r.at[j, side], at_core).wait_recv()

    def x1(j, d):
        return rc(dw.at[j, d, (x + 2) % 4], xr1.at[j, d], x1_s.at[j, d], x1_r.at[j, d], at_x(STEP[d]))

    def x2(j, d):
        return rc(dw.at[j, :, (x + STEP[d]) % 4], xr2.at[j, d], x2_s.at[j, d], x2_r.at[j, d], at_x(STEP[d]))

    def forward(j):
        for a, w in enumerate((w1t, wo)):
            part = nt(w[j].reshape(FC, DM), xg[a]).astype(BF16)
            for q in range(4):
                pu[j, q // 2, q % 2, a] = part[q * Q:(q + 1) * Q]
        core_copy(j).start()

    def place(side):
        return zl if side == 0 else 3 - zl

    def add_core(j):
        core_copy(j).wait_recv()
        pu[j, c] = (pu[j, c].astype(F32) + crecv[j].astype(F32)).astype(BF16)
        for side in range(2):
            @pl.when(place(side) == FAR)
            def _():
                for a in range(2):
                    chain(j, side, a).start()
                for a in range(2):
                    near(j, 1 - side, a).start()

    def pass_on(j, side):
        for a in range(2):
            chain(j, side, a).wait_recv()
            pu[j, c, side, a] = (pu[j, c, side, a].astype(F32) + zrecv[j, side, 1, a].astype(F32)).astype(BF16)
            chain(j, side, a).start()

    def finish(j, side):
        total = []
        for a in range(2):
            chain(j, side, a).wait_recv()
            near(j, side, a).wait_recv()
            total.append(
                pu[j, c, side, a].astype(F32) + zrecv[j, side, 0, a].astype(F32) + zrecv[j, side, 1, a].astype(F32)
            )
        for a, value in enumerate(activate(*total)):
            ah[j, a, 2 * c + side] = value
        for a in range(2):
            spread(j, side, a).start()
        for a in range(2):
            spread_near(j, side, a).start()
        core_share(j, side).start()

    def pass_back(j, side):
        for a in range(2):
            spread(j, side, a).wait_recv()
            spread(j, side, a).start()
        core_share(j, side).start()

    def take_far(j, side):
        for a in range(2):
            spread(j, side, a).wait_recv()
        core_share(j, side).start()

    def take_near(j, side):
        for a in range(2):
            spread_near(j, side, a).wait_recv()
        core_share(j, side).start()

    def backward(j):
        for side in range(2):
            core_share_wait(j, side)
        hidden_grad = ah[j, 1].reshape(FC, TOK)
        dw[j, 0] = nn(hidden_grad, xg[0]).astype(BF16).reshape(4, Q, DM)
        x1(j, 0).start()
        dw[j, 1] = nn(ah[j, 0].reshape(FC, TOK), xg[1]).astype(BF16).reshape(4, Q, DM)
        x1(j, 1).start()
        ng[...] += tn(hidden_grad, w1t[j].reshape(FC, DM))

    def x_step2(j):
        for d in range(2):
            x1(j, d).wait_recv()
            to = (x + STEP[d]) % 4
            dw[j, d, to] = (dw[j, d, to].astype(F32) + xr1[j, d].astype(F32)).astype(BF16)
            x2(j, d).start()

    def x_step3(j):
        for d in range(2):
            x2(j, d).wait_recv()
        rows = pl.ds(pl.multiple_of(j * Q, Q), Q)
        for a, out in enumerate((win_out, wout_out)):
            out[rows] = dw[j, a, x].astype(F32) + xr2[j, 0, a].astype(F32) + xr2[j, 1, a].astype(F32)

    def step(tau, carry):
        def stage(s, run, on=None):
            j = tau - s
            here = (j >= 0) & (j < NC)
            if on is not None:
                here = here & (place(on[0]) == on[1])

            @pl.when(here)
            def _():
                run(j)

        for side in range(2):
            stage(5, lambda j: take_far(j, side), (side, FAR))
            stage(4, lambda j: pass_back(j, side), (side, RELAY))
            stage(4, lambda j: take_near(j, side), (side, NEAR))
        for side in range(2):
            stage(3, lambda j: finish(j, side), (side, OWNER))
        for side in range(2):
            stage(2, lambda j: pass_on(j, side), (side, RELAY))
        stage(1, add_core)
        stage(0, forward)
        stage(S_BWD, backward)
        stage(S_X2, x_step2)
        stage(S_X3, x_step3)
        return carry

    lax.fori_loop(0, NC + S_BWD, step, 0)

    for h in range(2):
        ngb[:, :, h] = ng[:, h * HALF:(h + 1) * HALF].astype(BF16).reshape(4, 4, ROWS, HALF)

    def y1(k, d):
        return rc(ngb.at[(zh + k) % 4, (y + 2) % 4, d], yr1.at[k, d], gy1_s.at[k, d], gy1_r.at[k, d], at_y(STEP[d]))

    def y2(k, d):
        to = ngb.at[(zh + k) % 4, (y + STEP[d]) % 4]
        return rc(to, yr2.at[k, d], gy2_s.at[k, d], gy2_r.at[k, d], at_y(STEP[d]))

    def z1(d):
        return rc(zs.at[2, d], gz1.at[d], gz1_s.at[d], gz1_r.at[d], at_zh(STEP[d]))

    def z2(d):
        return rc(zs.at[STEP[d]], gz2.at[d], gz2_s.at[d], gz2_r.at[d], at_zh(STEP[d]))

    def along_y1(k):
        for d in range(2):
            y1(k, d).start()

    def along_y2(k):
        for d in range(2):
            y1(k, d).wait_recv()
            zz, to = (zh + k) % 4, (y + STEP[d]) % 4
            ngb[zz, to, d] = (ngb[zz, to, d].astype(F32) + yr1[k, d].astype(F32)).astype(BF16)
            y2(k, d).start()

    def sum_y(k):
        for d in range(2):
            y2(k, d).wait_recv()
        total = ngb[(zh + k) % 4, y].astype(F32) + yr2[k, 0].astype(F32) + yr2[k, 1].astype(F32)
        zs[k] = total.astype(BF16)

    for k in (2, 1, 3, 0):
        along_y1(k)
    along_y2(2)
    for k in (1, 3):
        along_y2(k)
    x_step2(NC - 1)
    sum_y(2)
    for d in range(2):
        z1(d).start()
    along_y2(0)
    for k in (1, 3):
        sum_y(k)
    x_step3(NC - 2)
    for d in range(2):
        z1(d).wait_recv()
        k = STEP[d]
        zs[k, d] = (zs[k, d].astype(F32) + gz1[d].astype(F32)).astype(BF16)
        z2(d).start()
    sum_y(0)
    x_step3(NC - 1)
    for d in range(2):
        z2(d).wait_recv()
    total = zs[0].astype(F32) + gz2[0].astype(F32) + gz2[1].astype(F32)
    for h in range(2):
        ng_out[:, h * HALF:(h + 1) * HALF] = total[h].astype(BF16)

    for d in range(2):
        for r in range(2):
            for a in range(2):
                az(d, a, r).wait_send()
            azf(d, r).wait_send()
            for k in range(4):
                for a in range(2):
                    ay(k, d, a, r).wait_send()
                ayf(k, d, r).wait_send()
        for k in range(4):
            y1(k, d).wait_send()
            y2(k, d).wait_send()
        z1(d).wait_send()
        z2(d).wait_send()

    def sent(j, carry):
        core_copy(j).wait_send()
        for side in range(2):
            here = place(side)
            for a in range(2):
                @pl.when(here == NEAR)
                def _():
                    near(j, side, a).wait_send()

                @pl.when(here >= RELAY)
                def _():
                    chain(j, side, a).wait_send()

                @pl.when(here == OWNER)
                def _():
                    spread_near(j, side, a).wait_send()

                @pl.when((here == OWNER) | (here == RELAY))
                def _():
                    spread(j, side, a).wait_send()

            core_share(j, side).wait_send()
            x1(j, side).wait_send()
            x2(j, side).wait_send()
        return carry

    lax.fori_loop(0, NC, sent, 0)


def write_out(*refs):
    sources, results, sem = refs[:3], refs[3:6], refs[6]
    copies = [pltpu.make_async_copy(s, r, sem.at[n]) for n, (s, r) in enumerate(zip(sources, results))]
    for copy in copies:
        copy.start()
    for copy in copies:
        copy.wait()


def per_device(normed, cotangent, w_in, w_out):
    vmem = pl.BlockSpec(memory_space=pltpu.VMEM)
    hbm = pl.BlockSpec(memory_space=pltpu.HBM)
    two = lambda *shape: [pltpu.SemaphoreType.DMA(shape)] * 2
    ng, win_t, wout = pl.pallas_call(
        kernel,
        out_shape=(
            jax.ShapeDtypeStruct((ROWS, DM), BF16),
            jax.ShapeDtypeStruct((FH // 4, DM), F32),
            jax.ShapeDtypeStruct((FH // 4, DM), F32),
        ),
        in_specs=[hbm, hbm, hbm, hbm],
        out_specs=[vmem, vmem, vmem],
        scratch_shapes=[
            pltpu.VMEM((2, TOK, DM), BF16),
            pltpu.VMEM((DM, FH), BF16),
            pltpu.VMEM((NC, 4, Q, DM), BF16),
            pltpu.VMEM((NC, 4, Q, DM), BF16),
            pltpu.VMEM((NC, 2, 2, 2, Q, TOK), BF16),
            pltpu.VMEM((NC, 2, 2, Q, TOK), BF16),
            pltpu.VMEM((NC, 2, 2, 2, Q, TOK), BF16),
            pltpu.VMEM((NC, 2, 4, Q, TOK), BF16),
            pltpu.VMEM((NC, 2, 4, Q, DM), BF16),
            pltpu.VMEM((NC, 2, Q, DM), BF16),
            pltpu.VMEM((NC, 2, 2, Q, DM), BF16),
            pltpu.VMEM((TOK, DM), F32),
            pltpu.VMEM((4, 4, 2, ROWS, HALF), BF16),
            pltpu.VMEM((4, 2, ROWS, HALF), BF16),
            pltpu.VMEM((4, 2, 2, ROWS, HALF), BF16),
            pltpu.VMEM((4, 2, ROWS, HALF), BF16),
            pltpu.VMEM((2, ROWS, HALF), BF16),
            pltpu.VMEM((2, 2, ROWS, HALF), BF16),
            pltpu.SemaphoreType.DMA((7,)),
            *two(2, 2, 2), *two(2, 2), *two(4, 2, 2, 2), *two(4, 2, 2),
            *two(NC), *two(NC, 2, 2), *two(NC, 2, 2), *two(NC, 2, 2), *two(NC, 2, 2), *two(NC, 2), *two(NC, 2), *two(NC, 2),
            *two(4, 2), *two(4, 2), *two(2), *two(2),
        ],
        compiler_params=pltpu.CompilerParams(
            collective_id=0, has_side_effects=True, vmem_limit_bytes=48 * 1024 * 1024
        ),
        name="mlp_branch",
    )(*[pltpu.with_memory_space_constraint(t, pltpu.HBM) for t in (normed, cotangent, w_in, w_out.reshape(4, NC, Q, DM))])
    sums = (ng, win_t, wout)
    ng, win_t, wout = pl.pallas_call(
        write_out,
        out_shape=[jax.ShapeDtypeStruct(s.shape, s.dtype) for s in sums],
        in_specs=[vmem] * 3,
        out_specs=[hbm] * 3,
        scratch_shapes=[pltpu.SemaphoreType.DMA((3,))],
        name="write_out",
    )(*sums)
    return ng, win_t.T, wout


def solution(mesh):
    return jax.shard_map(
        per_device,
        mesh=mesh,
        in_specs=(P(("dp", "mx"), "my"), P(("dp", "mx"), "my"), P("my", "mx"), P("mx", "my")),
        out_specs=(P(("dp", "mx"), "my"), P("my", ("mx", "dp")), P(("mx", "dp"), "my")),
        check_vma=False,
    )
```

time: 118 us -> 108 us (0.915)
  the two profiles are of different devices: /device:TPU:8 before, /device:TPU:32 now
where the time goes in v2:
time: 108 us
  Pallas kernels  105 us (97%)
  local copies, waits for them, and re-layouts  2.27 us (2%)
    pallas_call x1, Pallas kernels, per_device(): pl.pallas_call(kernel, out_shape=(jax.ShapeDtypeStruct((ROWS, DM), BF16),...  102 us
    pallas_call x1, Pallas kernels, per_device(): pl.pallas_call(write_out, out_shape=[jax.ShapeDtypeStruct(s.shape, s.dtyp...  2.31 us
    unnamed x6, local copies, waits for them, and re-layouts  2.27 us

profile of v2, /device:TPU:32, one launch (start us, length us, event | category | flops | bytes accessed | tf_op | source)
XLA Modules:
  0.0 107.7 jit_solution(13746557185215870686)
XLA Ops:
  0.6 102.4 %mlp_branch.1 = (bf16[32,768]{1,0:T(8,128)(2,1)S(1)}, f32[192,768]{1,0:T(8,128)S(1)}, f32[192,768]{1,0:T(8,128)S(1)}) custom-call(bf16[32,768]{1,0:T(8,128)(2,1)} %normed.1, bf16[32,768]{1,0:T(8,128)(2,1)} %cotangent.1, bf16[768,768]{1,0:T(8,128)(2,1)} %w_in.1, bf16[4,6,32,768]{3,2,1,0:T(8,128)(2,1)} %bitcast.2), custom_call_target="tpu_custom_call" | custom-call | tf_op jit(solution)/shard_map/mlp_branch/pallas_call | solution.py:455
  103.1 0.0 copy-start
  103.1 0.8 copy-done
  103.9 0.0 copy-start.1
  103.9 0.8 copy-done.1
  104.7 0.0 copy-start.2
  104.7 0.6 copy-done.2
  105.4 2.3 %write_out.1 = (bf16[32,768]{1,0:T(8,128)(2,1)}, f32[192,768]{1,0:T(8,128)}, f32[192,768]{1,0:T(8,128)}) custom-call(bf16[32,768]{1,0:T(8,128)(2,1)} %copy-done.2, f32[192,768]{1,0:T(8,128)} %copy-done, f32[192,768]{1,0:T(8,128)} %copy-done.1), custom_call_target="tpu_custom_call" | custom-call | tf_op jit(solution)/shard_map/write_out/pallas_call | solution.py:494
Async XLA Ops:
  103.1 0.8 copy-start
  103.9 0.8 copy-start.1
  104.7 0.6 copy-start.2

commit v3 on v0

v3 whole, which is shorter than its diff:
```python
import jax
import jax.numpy as jnp
from jax import lax
from jax.experimental import pallas as pl
from jax.experimental.pallas import tpu as pltpu
from jax.sharding import PartitionSpec as P

MESH = pl.DeviceIdType.MESH
BF16, F32 = jnp.bfloat16, jnp.float32

NC = 3
ROWS = 32
PIECE = ROWS // 2
GROUP = 4 * ROWS
TOK = 4 * GROUP
DM = 768
FH = 768
FC = FH // NC
Q = FC // 4
HALF = DM // 2

K_OF_P = (0, 3, 1, 2)
P_OF_K = (0, 2, 3, 1)
STEP = (1, 3)

START = (0, 5, 8, 11)
STEPS = START[3] + NC + 5


def nt(a, b):
    return lax.dot_general(a, b, (((1,), (1,)), ((), ())), preferred_element_type=F32)


def nn(a, b):
    return lax.dot_general(a, b, (((1,), (0,)), ((), ())), preferred_element_type=F32)


def tn(a, b):
    return lax.dot_general(a, b, (((0,), (0,)), ((), ())), preferred_element_type=F32)


def activate(preact, upstream):
    cumulative = 0.5 * (1.0 + lax.erf(preact * 0.7071067811865476))
    density = jnp.exp(-0.5 * preact * preact) * 0.3989422804014327
    activation = (preact * cumulative).astype(BF16)
    hidden_grad = (upstream * (cumulative + preact * density)).astype(BF16)
    return activation, hidden_grad


def kernel(
    normed, cotangent, w_in, w_out,
    ng_out, win_out, wout_out,
    xg, win_v, w1t, wo, pu, crecv, zrecv, ah, dw, xr1, xr2, ngb, yr1, yr2, zs, gz1, gz2,
    lsem, az_s, az_r, azf_s, azf_r, ay_s, ay_r, ayf_s, ayf_r,
    co_s, co_r, ne_s, ne_r, ch_s, ch_r, sn_s, sn_r, sp_s, sp_r, ce_s, ce_r, x1_s, x1_r, x2_s, x2_r,
    gy1_s, gy1_r, gy2_s, gy2_r, gz1_s, gz1_r, gz2_s, gz2_r,
):
    x = lax.axis_index("dp")
    mx = lax.axis_index("mx")
    my = lax.axis_index("my")
    zh, y = mx // 4, mx % 4
    zl, c = my // 2, my % 2
    o = 1 - c

    def at_x(k):
        return {"dp": (x + k) % 4}

    def at_y(k):
        return {"mx": zh * 4 + (y + k) % 4}

    def at_zh(k):
        return {"mx": ((zh + k) % 4) * 4 + y}

    def at_zl(k):
        return {"my": ((zl + k) % 4) * 2 + c}

    at_core = {"my": zl * 2 + o}

    def rc(src, dst, send, recv, device):
        return pltpu.make_async_remote_copy(
            src_ref=src, dst_ref=dst, send_sem=send, recv_sem=recv, device_id=device, device_id_type=MESH
        )

    load_own = [pltpu.make_async_copy(t, xg.at[a, 0, 0], lsem.at[5 + a]) for a, t in enumerate((normed, cotangent))]
    load_in = pltpu.make_async_copy(w_in, win_v, lsem.at[4])
    load_out = [pltpu.make_async_copy(w_out.at[g], wo.at[:, g], lsem.at[g]) for g in range(4)]
    for copy in (*load_own, load_in, *load_out):
        copy.start()

    barrier = pltpu.get_barrier_semaphore()
    partners = [at_core]
    for k in (1, 3):
        partners += [at_x(k), at_y(k), at_zh(k), at_zl(k)]
    for device in partners:
        pl.semaphore_signal(barrier, inc=1, device_id=device, device_id_type=MESH)
    pl.semaphore_wait(barrier, len(partners))

    def rows(a, p, yy, r):
        return xg.at[a, p, yy, pl.ds(r * PIECE, PIECE)]

    def az(d, a, r):
        there = rows(a, P_OF_K[STEP[1 - d]], 0, r)
        return rc(rows(a, 0, 0, r), there, az_s.at[d, a, r], az_r.at[d, a, r], at_zh(STEP[d]))

    def azf(d, r):
        here = rows(d, P_OF_K[STEP[1 - d]], 0, r)
        return rc(here, rows(d, 3, 0, r), azf_s.at[d, r], azf_r.at[d, r], at_zh(STEP[d]))

    def ay(p, d, a, r):
        there = rows(a, p, STEP[1 - d], r)
        return rc(rows(a, p, 0, r), there, ay_s.at[p, d, a, r], ay_r.at[p, d, a, r], at_y(STEP[d]))

    def ayf(p, d, r):
        here = rows(d, p, STEP[1 - d], r)
        return rc(here, rows(d, p, 2, r), ayf_s.at[p, d, r], ayf_r.at[p, d, r], at_y(STEP[d]))

    def along_y(p, a, r):
        for d in range(2):
            ay(p, d, a, r).start()

    def further_y(p, a, r):
        ay(p, a, a, r).wait_recv()
        ayf(p, a, r).start()

    def group_here(p):
        for d in range(2):
            for r in range(2):
                ay(p, d, 1 - d, r).wait_recv()
                ayf(p, d, r).wait_recv()

    for copy in load_own:
        copy.wait()
    for a in range(2):
        for r in range(2):
            az(0, a, r).start()
            az(1, 1 - a, r).start()
            ay(0, 0, a, r).start()
            ay(0, 1, 1 - a, r).start()

    load_in.wait()
    for k in range(FH // 128):
        turned = win_v[:, k * 128:(k + 1) * 128].T
        for u in range(0, 128, 32):
            g, rest = divmod(k * 128 + u, FH // 4)
            w1t[rest // Q, g, pl.ds(rest % Q, 32)] = turned[u:u + 32]
    for copy in load_out:
        copy.wait()

    for r in range(2):
        for a in range(2):
            further_y(0, a, r)

    WAVES = [[(0, 0, r), (1, 1, r)] for r in range(2)] + [[(0, 1, r), (1, 0, r)] for r in range(2)]

    def wave(w):
        if w < 4:
            for d, a, r in WAVES[w]:
                az(d, a, r).wait_recv()
                if d == a:
                    azf(d, r).start()
                along_y(P_OF_K[STEP[1 - d]], a, r)
        else:
            for d in range(2):
                azf(d, w - 4).wait_recv()
                along_y(3, d, w - 4)

    def wave_on(w):
        if w < 4:
            for d, a, r in WAVES[w]:
                further_y(P_OF_K[STEP[1 - d]], a, r)
        else:
            for d in range(2):
                further_y(3, d, w - 4)

    group_here(0)

    NEAR, OWNER, RELAY, FAR = range(4)

    def place(side):
        return zl if side == 0 else 3 - zl

    def core_copy(j, p):
        return rc(pu.at[j, p, o], crecv.at[j, p], co_s.at[j, p], co_r.at[j, p], at_core)

    def near(j, p, side):
        there = zrecv.at[j, p, side, 0]
        return rc(pu.at[j, p, c, side], there, ne_s.at[j, p, side], ne_r.at[j, p, side], at_zl(STEP[side]))

    def chain(j, p, side):
        there = zrecv.at[j, p, side, 1]
        return rc(pu.at[j, p, c, side], there, ch_s.at[j, p, side], ch_r.at[j, p, side], at_zl(STEP[1 - side]))

    def spread_near(j, p, side):
        here = ah.at[:, j, p, 2 * c + side]
        return rc(here, here, sn_s.at[j, p, side], sn_r.at[j, p, side], at_zl(STEP[1 - side]))

    def spread(j, p, side):
        here = ah.at[:, j, p, 2 * c + side]
        return rc(here, here, sp_s.at[j, p, side], sp_r.at[j, p, side], at_zl(STEP[side]))

    def core_share(j, p, side):
        here = ah.at[:, j, p, 2 * c + side]
        return rc(here, here, ce_s.at[j, p, side], ce_r.at[j, p, side], at_core)

    def core_share_wait(j, p, side):
        here = ah.at[:, j, p, 2 * o + side]
        rc(here, here, ce_s.at[j, p, side], ce_r.at[j, p, side], at_core).wait_recv()

    def x1(j, d):
        return rc(dw.at[j, d, (x + 2) % 4], xr1.at[j, d], x1_s.at[j, d], x1_r.at[j, d], at_x(STEP[d]))

    def x2(j, d):
        return rc(dw.at[j, :, (x + STEP[d]) % 4], xr2.at[j, d], x2_s.at[j, d], x2_r.at[j, d], at_x(STEP[d]))

    def y1(p, d):
        return rc(ngb.at[p, 2, d], yr1.at[p, d], gy1_s.at[p, d], gy1_r.at[p, d], at_y(STEP[d]))

    def y2(p, d):
        return rc(ngb.at[p, STEP[d]], yr2.at[p, d], gy2_s.at[p, d], gy2_r.at[p, d], at_y(STEP[d]))

    def z1(d):
        return rc(zs.at[3, d], gz1.at[d], gz1_s.at[d], gz1_r.at[d], at_zh(STEP[d]))

    def z2(d):
        return rc(zs.at[P_OF_K[STEP[d]]], gz2.at[d], gz2_s.at[d], gz2_r.at[d], at_zh(STEP[d]))

    def forward(j, p):
        for a, w in enumerate((w1t, wo)):
            part = nt(w[j].reshape(FC, DM), xg[a, p].reshape(GROUP, DM)).astype(BF16)
            for q in range(4):
                pu[j, p, q // 2, q % 2, a] = part[q * Q:(q + 1) * Q]
        core_copy(j, p).start()

    def add_core(j, p):
        core_copy(j, p).wait_recv()
        pu[j, p, c] = (pu[j, p, c].astype(F32) + crecv[j, p].astype(F32)).astype(BF16)
        for side in range(2):
            @pl.when(place(side) == FAR)
            def _():
                chain(j, p, side).start()
                near(j, p, 1 - side).start()

    def pass_on(j, p, side):
        chain(j, p, side).wait_recv()
        pu[j, p, c, side] = (pu[j, p, c, side].astype(F32) + zrecv[j, p, side, 1].astype(F32)).astype(BF16)
        chain(j, p, side).start()

    def finish(j, p, side):
        near(j, p, side).wait_recv()
        chain(j, p, side).wait_recv()
        total = pu[j, p, c, side].astype(F32) + zrecv[j, p, side, 0].astype(F32) + zrecv[j, p, side, 1].astype(F32)
        for a, value in enumerate(activate(total[0], total[1])):
            ah[a, j, p, 2 * c + side] = value
        spread(j, p, side).start()
        spread_near(j, p, side).start()
        core_share(j, p, side).start()

    def pass_back(j, p, side):
        spread(j, p, side).wait_recv()
        spread(j, p, side).start()
        core_share(j, p, side).start()

    def take_far(j, p, side):
        spread(j, p, side).wait_recv()
        core_share(j, p, side).start()

    def take_near(j, p, side):
        spread_near(j, p, side).wait_recv()
        core_share(j, p, side).start()

    def units(a, j):
        return jnp.concatenate([ah[a, j, p].reshape(FC, GROUP) for p in range(4)], axis=1)

    def backward(j, p):
        for side in range(2):
            core_share_wait(j, p, side)

        @pl.when(p == 3)
        def _():
            for d in range(2):
                dw[j, d] = nn(units(1 - d, j), xg[d].reshape(TOK, DM)).astype(BF16).reshape(4, Q, DM)
                x1(j, d).start()

        @pl.when(j == NC - 1)
        def _():
            total = tn(ah[1, :, p].reshape(FH, GROUP), w1t[...].reshape(FH, DM)).astype(BF16)
            for h in range(2):
                ngb[p, :, h] = total[:, h * HALF:(h + 1) * HALF].reshape(4, ROWS, HALF)
            for d in range(2):
                y1(p, d).start()

    def x_step2(j):
        for d in range(2):
            x1(j, d).wait_recv()
            to = (x + STEP[d]) % 4
            dw[j, d, to] = (dw[j, d, to].astype(F32) + xr1[j, d].astype(F32)).astype(BF16)
            x2(j, d).start()

    def x_step3(j):
        for d in range(2):
            x2(j, d).wait_recv()
        for a, out in enumerate((win_out, wout_out)):
            out[j * Q:(j + 1) * Q] = dw[j, a, x].astype(F32) + xr2[j, 0, a].astype(F32) + xr2[j, 1, a].astype(F32)

    def along_y2(p):
        for d in range(2):
            y1(p, d).wait_recv()
            ngb[p, STEP[d], d] = (ngb[p, STEP[d], d].astype(F32) + yr1[p, d].astype(F32)).astype(BF16)
            y2(p, d).start()

    def sum_y(p):
        for d in range(2):
            y2(p, d).wait_recv()
        zs[p] = (ngb[p, 0].astype(F32) + yr2[p, 0].astype(F32) + yr2[p, 1].astype(F32)).astype(BF16)

    AHEAD = {0: [0, 1], 1: [2], 2: [3], 3: [4], 4: [5]}
    AFTER = {0: [0], 1: [1], 2: [2], 3: [3], 4: [4], 5: [5]}

    def step(tau, carry):
        def stage(s, run, on=None):
            slot = tau - s
            p = sum(jnp.where(slot >= START[i], 1, 0) for i in range(1, 4))
            first = sum(jnp.where(slot >= START[i], START[i] - START[i - 1], 0) for i in range(1, 4))
            j = slot - first
            here = (slot >= 0) & (j < NC)
            if on is not None:
                here = here & (place(on[0]) == on[1])

            @pl.when(here)
            def _():
                run(j, p)

        def at(n, run):
            @pl.when(tau == n)
            def _():
                run()

        for n, waves in AHEAD.items():
            at(n, lambda: [wave(w) for w in waves])
        for side in range(2):
            stage(5, lambda j, p: take_far(j, p, side), (side, FAR))
            stage(4, lambda j, p: pass_back(j, p, side), (side, RELAY))
            stage(4, lambda j, p: take_near(j, p, side), (side, NEAR))
        for side in range(2):
            stage(3, lambda j, p: finish(j, p, side), (side, OWNER))
        for side in range(2):
            stage(2, lambda j, p: pass_on(j, p, side), (side, RELAY))
        stage(1, add_core)
        for n, waves in AFTER.items():
            at(n, lambda: [wave_on(w) for w in waves])
        for p in range(1, 4):
            at(START[p], lambda: group_here(p))
        stage(0, forward)
        stage(5, backward)
        for p in range(3):
            at(START[p] + NC - 1 + 7, lambda: along_y2(p))
            at(START[p] + NC - 1 + 9, lambda: sum_y(p))
        return carry

    lax.fori_loop(0, STEPS, step, 0)

    x_step2(0)
    for p in range(3):
        if START[p] + NC - 1 + 7 >= STEPS:
            along_y2(p)
    x_step2(1)
    along_y2(3)
    for j in range(2, NC):
        x_step2(j)
    for p in range(3):
        if START[p] + NC - 1 + 9 >= STEPS:
            sum_y(p)
    sum_y(3)
    for d in range(2):
        z1(d).start()
    for j in range(NC - 2):
        x_step3(j)
    for d in range(2):
        z1(d).wait_recv()
        p = P_OF_K[STEP[d]]
        zs[p, d] = (zs[p, d].astype(F32) + gz1[d].astype(F32)).astype(BF16)
        z2(d).start()
    x_step3(NC - 2)
    for d in range(2):
        z2(d).wait_recv()
    total = zs[0].astype(F32) + gz2[0].astype(F32) + gz2[1].astype(F32)
    for h in range(2):
        ng_out[:, h * HALF:(h + 1) * HALF] = total[h].astype(BF16)
    x_step3(NC - 1)

    for d in range(2):
        for r in range(2):
            for a in range(2):
                az(d, a, r).wait_send()
            azf(d, r).wait_send()
            for p in range(4):
                for a in range(2):
                    ay(p, d, a, r).wait_send()
                ayf(p, d, r).wait_send()
        for p in range(4):
            y1(p, d).wait_send()
            y2(p, d).wait_send()
        for j in range(NC):
            x1(j, d).wait_send()
            x2(j, d).wait_send()
        z1(d).wait_send()
        z2(d).wait_send()

    def sent(u, carry):
        j, p = u % NC, u // NC
        core_copy(j, p).wait_send()
        for side in range(2):
            here = place(side)

            @pl.when(here == NEAR)
            def _():
                near(j, p, side).wait_send()

            @pl.when(here >= RELAY)
            def _():
                chain(j, p, side).wait_send()

            @pl.when(here == OWNER)
            def _():
                spread_near(j, p, side).wait_send()

            @pl.when((here == OWNER) | (here == RELAY))
            def _():
                spread(j, p, side).wait_send()

            core_share(j, p, side).wait_send()
        return carry

    lax.fori_loop(0, 4 * NC, sent, 0)


def per_device(normed, cotangent, w_in, w_out):
    vmem = pl.BlockSpec(memory_space=pltpu.VMEM)
    hbm = pl.BlockSpec(memory_space=pltpu.HBM)
    two = lambda *shape: [pltpu.SemaphoreType.DMA(shape)] * 2
    inputs = (normed, cotangent, w_in, w_out.reshape(4, NC, Q, DM))
    ng, win_t, wout = pl.pallas_call(
        kernel,
        out_shape=(
            jax.ShapeDtypeStruct((ROWS, DM), BF16),
            jax.ShapeDtypeStruct((FH // 4, DM), F32),
            jax.ShapeDtypeStruct((FH // 4, DM), F32),
        ),
        in_specs=[hbm, hbm, hbm, hbm],
        out_specs=[vmem, vmem, vmem],
        scratch_shapes=[
            pltpu.VMEM((2, 4, 4, ROWS, DM), BF16),
            pltpu.VMEM((DM, FH), BF16),
            pltpu.VMEM((NC, 4, Q, DM), BF16),
            pltpu.VMEM((NC, 4, Q, DM), BF16),
            pltpu.VMEM((NC, 4, 2, 2, 2, Q, GROUP), BF16),
            pltpu.VMEM((NC, 4, 2, 2, Q, GROUP), BF16),
            pltpu.VMEM((NC, 4, 2, 2, 2, Q, GROUP), BF16),
            pltpu.VMEM((2, NC, 4, 4, Q, GROUP), BF16),
            pltpu.VMEM((NC, 2, 4, Q, DM), BF16),
            pltpu.VMEM((NC, 2, Q, DM), BF16),
            pltpu.VMEM((NC, 2, 2, Q, DM), BF16),
            pltpu.VMEM((4, 4, 2, ROWS, HALF), BF16),
            pltpu.VMEM((4, 2, ROWS, HALF), BF16),
            pltpu.VMEM((4, 2, 2, ROWS, HALF), BF16),
            pltpu.VMEM((4, 2, ROWS, HALF), BF16),
            pltpu.VMEM((2, ROWS, HALF), BF16),
            pltpu.VMEM((2, 2, ROWS, HALF), BF16),
            pltpu.SemaphoreType.DMA((7,)),
            *two(2, 2, 2), *two(2, 2), *two(4, 2, 2, 2), *two(4, 2, 2),
            *two(NC, 4), *two(NC, 4, 2), *two(NC, 4, 2), *two(NC, 4, 2), *two(NC, 4, 2), *two(NC, 4, 2),
            *two(NC, 2), *two(NC, 2),
            *two(4, 2), *two(4, 2), *two(2), *two(2),
        ],
        compiler_params=pltpu.CompilerParams(
            collective_id=0, has_side_effects=True, vmem_limit_bytes=48 * 1024 * 1024
        ),
        name="mlp_branch",
    )(*[pltpu.with_memory_space_constraint(t, pltpu.HBM) for t in inputs])
    return ng, win_t.T, wout


def solution(mesh):
    return jax.shard_map(
        per_device,
        mesh=mesh,
        in_specs=(P(("dp", "mx"), "my"), P(("dp", "mx"), "my"), P("my", "mx"), P("mx", "my")),
        out_specs=(P(("dp", "mx"), "my"), P("my", ("mx", "dp")), P(("mx", "dp"), "my")),
        check_vma=False,
    )
```

time: 414 us -> 109 us (0.26)
  waiting for transfers between devices: 260 us -> 0 us
  blocking collectives: 121 us -> 0 us
  Pallas kernels: 0 us -> 106 us
  between operations: 13.8 us -> 0.64 us
  matrix products: 10 us -> 0 us
  other arithmetic: 4.37 us -> 0 us
    reduce_scatter x3 -> x0, waiting for transfers between devices: 173 us -> none  [the longest x1 115 us: per_device(): lax.psum_scatter(jnp.einsum('tf,df->td', hidden_grad, w_in, preferred_ele...]
    all_gather x2 -> x0, blocking collectives: 121 us -> none  [the longest x1 62.4 us: per_device(): lax.all_gather(normed, 'mx', axis=0, tiled=True)]
    pallas_call x0 -> x1, Pallas kernels: none -> 106 us  [per_device(): pl.pallas_call(kernel, out_shape=(jax.ShapeDtypeStruct((ROWS, DM), BF16),...]
    psum x1 -> x0, waiting for transfers between devices: 87.6 us -> none  [per_device(): lax.psum(pre_part.astype(jnp.bfloat16), 'my').astype(jnp.float32)]
    dot_general x5 -> x0, matrix products: 10 us -> none  [the longest x1 3.1 us: per_device(): jnp.einsum('tf,td->fd', activation, rows_g, preferred_element_type=jnp.fl...]
    convert_element_type x3 -> x0, other arithmetic: 4.37 us -> none  [the longest x2 3.63 us: per_device(): w_in_grad, w_out_grad = (lax.psum_scatter(in_term.astype(jnp.bfloat16), '...]
  transfers between devices with their start and end apart: 4 -> 0, of which waited for: 4 -> 0; matrix products, arithmetic and copies ran while one was open for 2% -> 0% of each run, Pallas kernels for 0% -> 0%
where the time goes in v3:
time: 109 us
  Pallas kernels  106 us (97%)
  local copies, waits for them, and re-layouts  2.25 us (2%)
    pallas_call x1, Pallas kernels, per_device(): pl.pallas_call(kernel, out_shape=(jax.ShapeDtypeStruct((ROWS, DM), BF16),...  106 us
    unnamed x3, local copies, waits for them, and re-layouts  2.25 us

profile of v3, /device:TPU:1, one launch (start us, length us, event | category | flops | bytes accessed | tf_op | source)
XLA Modules:
  0.0 109.2 jit_solution(15830910273470548595)
XLA Ops:
  0.6 106.3 %mlp_branch.1 = (bf16[32,768]{1,0:T(8,128)(2,1)S(1)}, f32[192,768]{1,0:T(8,128)S(1)}, f32[192,768]{1,0:T(8,128)S(1)}) custom-call(bf16[32,768]{1,0:T(8,128)(2,1)} %normed.1, bf16[32,768]{1,0:T(8,128)(2,1)} %cotangent.1, bf16[768,768]{1,0:T(8,128)(2,1)} %w_in.1, bf16[4,3,64,768]{3,2,1,0:T(8,128)(2,1)} %bitcast.3), custom_call_target="tpu_custom_call" | custom-call | tf_op jit(solution)/shard_map/mlp_branch/pallas_call | solution.py:442
  107.0 0.6 copy.10
  107.6 0.8 copy.11
  108.4 0.8 copy.12

commit v4 on v3

--- a/solution.py
+++ b/solution.py
@@ -23,8 +23,19 @@
 P_OF_K = (0, 2, 3, 1)
 STEP = (1, 3)
 
-START = (0, 5, 8, 11)
-STEPS = START[3] + NC + 5
+UNITS = ((0, 0), (0, 1), (0, 2), (1, 0), (2, 0), (1, 1), (3, 0), (3, 1), (3, 2), (2, 1), (1, 2), (2, 2))
+GROUP_CODE = sum(p << (2 * n) for n, (p, j) in enumerate(UNITS))
+CHUNK_CODE = sum(j << (2 * n) for n, (p, j) in enumerate(UNITS))
+GROUP_FIRST = [min(n for n, u in enumerate(UNITS) if u[0] == p) for p in range(4)]
+GROUP_LAST = [max(n for n, u in enumerate(UNITS) if u[0] == p) for p in range(4)]
+CHUNK_LAST = [max(n for n, u in enumerate(UNITS) if u[1] == j) for j in range(NC)]
+
+SP = 3
+S_ADD, S_RELAY, S_FINISH, S_BACK, S_FAR = 1, 1 + SP, 1 + 2 * SP, 1 + 3 * SP, 1 + 4 * SP
+S_BWD = S_FAR + 1
+STEPS = len(UNITS) + S_BWD
+X_STEP2 = 3
+Y_STEP2, Y_SUM = 2, 5
 
 
 def nt(a, b):
@@ -60,7 +71,6 @@
     my = lax.axis_index("my")
     zh, y = mx // 4, mx % 4
     zl, c = my // 2, my % 2
-    o = 1 - c
 
     def at_x(k):
         return {"dp": (x + k) % 4}
@@ -74,7 +84,7 @@
     def at_zl(k):
         return {"my": ((zl + k) % 4) * 2 + c}
 
-    at_core = {"my": zl * 2 + o}
+    at_core = {"my": zl * 2 + 1 - c}
 
     def rc(src, dst, send, recv, device):
         return pltpu.make_async_remote_copy(
@@ -145,10 +155,6 @@
             w1t[rest // Q, g, pl.ds(rest % Q, 32)] = turned[u:u + 32]
     for copy in load_out:
         copy.wait()
-
-    for r in range(2):
-        for a in range(2):
-            further_y(0, a, r)
 
     WAVES = [[(0, 0, r), (1, 1, r)] for r in range(2)] + [[(0, 1, r), (1, 0, r)] for r in range(2)]
 
@@ -172,7 +178,20 @@
             for d in range(2):
                 further_y(3, d, w - 4)
 
+    for r in range(2):
+        for a in range(2):
+            further_y(0, a, r)
+    wave(0)
+    wave(1)
+    wave(2)
+    wave_on(0)
     group_here(0)
+    wave(3)
+    wave_on(1)
+    wave(4)
+    wave_on(2)
+    wave(5)
+    wave_on(3)
 
     NEAR, OWNER, RELAY, FAR = range(4)
 
@@ -180,31 +199,27 @@
         return zl if side == 0 else 3 - zl
 
     def core_copy(j, p):
-        return rc(pu.at[j, p, o], crecv.at[j, p], co_s.at[j, p], co_r.at[j, p], at_core)
+        return rc(pu.at[j, p], crecv.at[j, p], co_s.at[j, p], co_r.at[j, p], at_core)
 
     def near(j, p, side):
         there = zrecv.at[j, p, side, 0]
-        return rc(pu.at[j, p, c, side], there, ne_s.at[j, p, side], ne_r.at[j, p, side], at_zl(STEP[side]))
+        return rc(pu.at[j, p, side], there, ne_s.at[j, p, side], ne_r.at[j, p, side], at_zl(STEP[side]))
 
     def chain(j, p, side):
         there = zrecv.at[j, p, side, 1]
-        return rc(pu.at[j, p, c, side], there, ch_s.at[j, p, side], ch_r.at[j, p, side], at_zl(STEP[1 - side]))
+        return rc(pu.at[j, p, side], there, ch_s.at[j, p, side], ch_r.at[j, p, side], at_zl(STEP[1 - side]))
 
     def spread_near(j, p, side):
-        here = ah.at[:, j, p, 2 * c + side]
+        here = ah.at[:, j, p, side]
         return rc(here, here, sn_s.at[j, p, side], sn_r.at[j, p, side], at_zl(STEP[1 - side]))
 
     def spread(j, p, side):
-        here = ah.at[:, j, p, 2 * c + side]
+        here = ah.at[:, j, p, side]
         return rc(here, here, sp_s.at[j, p, side], sp_r.at[j, p, side], at_zl(STEP[side]))
 
     def core_share(j, p, side):
-        here = ah.at[:, j, p, 2 * c + side]
+        here = ah.at[:, j, p, side]
         return rc(here, here, ce_s.at[j, p, side], ce_r.at[j, p, side], at_core)
-
-    def core_share_wait(j, p, side):
-        here = ah.at[:, j, p, 2 * o + side]
-        rc(here, here, ce_s.at[j, p, side], ce_r.at[j, p, side], at_core).wait_recv()
 
     def x1(j, d):
         return rc(dw.at[j, d, (x + 2) % 4], xr1.at[j, d], x1_s.at[j, d], x1_r.at[j, d], at_x(STEP[d]))
@@ -227,13 +242,16 @@
     def forward(j, p):
         for a, w in enumerate((w1t, wo)):
             part = nt(w[j].reshape(FC, DM), xg[a, p].reshape(GROUP, DM)).astype(BF16)
-            for q in range(4):
-                pu[j, p, q // 2, q % 2, a] = part[q * Q:(q + 1) * Q]
-        core_copy(j, p).start()
+            for side in range(2):
+                pu[j, p, side, a] = part[side * 2 * Q:(side + 1) * 2 * Q]
+
+        @pl.when(c == 0)
+        def _():
+            core_copy(j, p).start()
 
     def add_core(j, p):
         core_copy(j, p).wait_recv()
-        pu[j, p, c] = (pu[j, p, c].astype(F32) + crecv[j, p].astype(F32)).astype(BF16)
+        pu[j, p] = (pu[j, p].astype(F32) + crecv[j, p].astype(F32)).astype(BF16)
         for side in range(2):
             @pl.when(place(side) == FAR)
             def _():
@@ -242,15 +260,15 @@
 
     def pass_on(j, p, side):
         chain(j, p, side).wait_recv()
-        pu[j, p, c, side] = (pu[j, p, c, side].astype(F32) + zrecv[j, p, side, 1].astype(F32)).astype(BF16)
+        pu[j, p, side] = (pu[j, p, side].astype(F32) + zrecv[j, p, side, 1].astype(F32)).astype(BF16)
         chain(j, p, side).start()
 
     def finish(j, p, side):
         near(j, p, side).wait_recv()
         chain(j, p, side).wait_recv()
-        total = pu[j, p, c, side].astype(F32) + zrecv[j, p, side, 0].astype(F32) + zrecv[j, p, side, 1].astype(F32)
+        total = pu[j, p, side].astype(F32) + zrecv[j, p, side, 0].astype(F32) + zrecv[j, p, side, 1].astype(F32)
         for a, value in enumerate(activate(total[0], total[1])):
-            ah[a, j, p, 2 * c + side] = value
+            ah[a, j, p, side] = value
         spread(j, p, side).start()
         spread_near(j, p, side).start()
         core_share(j, p, side).start()
@@ -271,23 +289,21 @@
     def units(a, j):
         return jnp.concatenate([ah[a, j, p].reshape(FC, GROUP) for p in range(4)], axis=1)
 
-    def backward(j, p):
+    def take_shares(j, p):
         for side in range(2):
-            core_share_wait(j, p, side)
-
-        @pl.when(p == 3)
-        def _():
-            for d in range(2):
-                dw[j, d] = nn(units(1 - d, j), xg[d].reshape(TOK, DM)).astype(BF16).reshape(4, Q, DM)
-                x1(j, d).start()
-
-        @pl.when(j == NC - 1)
-        def _():
-            total = tn(ah[1, :, p].reshape(FH, GROUP), w1t[...].reshape(FH, DM)).astype(BF16)
-            for h in range(2):
-                ngb[p, :, h] = total[:, h * HALF:(h + 1) * HALF].reshape(4, ROWS, HALF)
-            for d in range(2):
-                y1(p, d).start()
+            core_share(j, p, side).wait_recv()
+
+    def weight_grads(j, p):
+        for d in range(2):
+            dw[j, d] = nn(units(1 - d, j), xg[d].reshape(TOK, DM)).astype(BF16).reshape(4, Q, DM)
+            x1(j, d).start()
+
+    def normed_grad(j, p):
+        total = tn(ah[1, :, p].reshape(FH, GROUP), w1t[...].reshape(FH, DM)).astype(BF16)
+        for h in range(2):
+            ngb[p, :, h] = total[:, h * HALF:(h + 1) * HALF].reshape(4, ROWS, HALF)
+        for d in range(2):
+            y1(p, d).start()
 
     def x_step2(j):
         for d in range(2):
@@ -313,21 +329,22 @@
             y2(p, d).wait_recv()
         zs[p] = (ngb[p, 0].astype(F32) + yr2[p, 0].astype(F32) + yr2[p, 1].astype(F32)).astype(BF16)
 
-    AHEAD = {0: [0, 1], 1: [2], 2: [3], 3: [4], 4: [5]}
-    AFTER = {0: [0], 1: [1], 2: [2], 3: [3], 4: [4], 5: [5]}
+    AFTER = {1: lambda: wave_on(4), 2: lambda: wave_on(5)}
 
     def step(tau, carry):
-        def stage(s, run, on=None):
+        def stage(s, run, on=None, core=None, among=None):
             slot = tau - s
-            p = sum(jnp.where(slot >= START[i], 1, 0) for i in range(1, 4))
-            first = sum(jnp.where(slot >= START[i], START[i] - START[i - 1], 0) for i in range(1, 4))
-            j = slot - first
-            here = (slot >= 0) & (j < NC)
+            here = (slot >= 0) & (slot < len(UNITS))
             if on is not None:
-                here = here & (place(on[0]) == on[1])
+                here = here & (c == 1) & (place(on[0]) == on[1])
+            if core is not None:
+                here = here & (c == core)
+            if among is not None:
+                here = sum(jnp.where(slot == n, 1, 0) for n in among) > 0
 
             @pl.when(here)
             def _():
+                j, p = ((code >> (2 * slot)) & 3 for code in (CHUNK_CODE, GROUP_CODE))
                 run(j, p)
 
         def at(n, run):
@@ -335,58 +352,69 @@
             def _():
                 run()
 
-        for n, waves in AHEAD.items():
-            at(n, lambda: [wave(w) for w in waves])
         for side in range(2):
-            stage(5, lambda j, p: take_far(j, p, side), (side, FAR))
-            stage(4, lambda j, p: pass_back(j, p, side), (side, RELAY))
-            stage(4, lambda j, p: take_near(j, p, side), (side, NEAR))
+            stage(S_FAR, lambda j, p: take_far(j, p, side), (side, FAR))
+            stage(S_BACK, lambda j, p: pass_back(j, p, side), (side, RELAY))
+            stage(S_BACK, lambda j, p: take_near(j, p, side), (side, NEAR))
         for side in range(2):
-            stage(3, lambda j, p: finish(j, p, side), (side, OWNER))
+            stage(S_FINISH, lambda j, p: finish(j, p, side), (side, OWNER))
         for side in range(2):
-            stage(2, lambda j, p: pass_on(j, p, side), (side, RELAY))
-        stage(1, add_core)
-        for n, waves in AFTER.items():
-            at(n, lambda: [wave_on(w) for w in waves])
+            stage(S_RELAY, lambda j, p: pass_on(j, p, side), (side, RELAY))
+        stage(S_ADD, add_core, core=1)
+        for n, run in AFTER.items():
+            at(n, run)
         for p in range(1, 4):
-            at(START[p], lambda: group_here(p))
+            at(GROUP_FIRST[p], lambda: group_here(p))
         stage(0, forward)
-        stage(5, backward)
-        for p in range(3):
-            at(START[p] + NC - 1 + 7, lambda: along_y2(p))
-            at(START[p] + NC - 1 + 9, lambda: sum_y(p))
+        stage(S_BWD, take_shares, core=0)
+        stage(S_BWD, weight_grads, among=CHUNK_LAST)
+        stage(S_BWD, normed_grad, among=GROUP_LAST)
+        for j in range(NC):
+            at(CHUNK_LAST[j] + S_BWD + X_STEP2, lambda: x_step2(j))
+        for p in range(4):
+            at(GROUP_LAST[p] + S_BWD + Y_STEP2, lambda: along_y2(p))
+            at(GROUP_LAST[p] + S_BWD + Y_SUM, lambda: sum_y(p))
         return carry
 
     lax.fori_loop(0, STEPS, step, 0)
 
-    x_step2(0)
-    for p in range(3):
-        if START[p] + NC - 1 + 7 >= STEPS:
+    def rest_x(j):
+        if CHUNK_LAST[j] + S_BWD + X_STEP2 >= STEPS:
+            x_step2(j)
+
+    def rest_y2(p):
+        if GROUP_LAST[p] + S_BWD + Y_STEP2 >= STEPS:
             along_y2(p)
-    x_step2(1)
-    along_y2(3)
-    for j in range(2, NC):
-        x_step2(j)
-    for p in range(3):
-        if START[p] + NC - 1 + 9 >= STEPS:
+
+    def rest_y(p):
+        if GROUP_LAST[p] + S_BWD + Y_SUM >= STEPS:
             sum_y(p)
-    sum_y(3)
+
+    rest_y2(3)
+    rest_y(0)
+    rest_x(0)
+    rest_y(3)
     for d in range(2):
         z1(d).start()
-    for j in range(NC - 2):
-        x_step3(j)
+    rest_y2(1)
+    rest_y2(2)
+    rest_x(1)
+    x_step3(0)
+    rest_y(1)
+    rest_x(2)
+    rest_y(2)
     for d in range(2):
         z1(d).wait_recv()
         p = P_OF_K[STEP[d]]
         zs[p, d] = (zs[p, d].astype(F32) + gz1[d].astype(F32)).astype(BF16)
         z2(d).start()
-    x_step3(NC - 2)
+    x_step3(1)
     for d in range(2):
         z2(d).wait_recv()
     total = zs[0].astype(F32) + gz2[0].astype(F32) + gz2[1].astype(F32)
     for h in range(2):
         ng_out[:, h * HALF:(h + 1) * HALF] = total[h].astype(BF16)
-    x_step3(NC - 1)
+    x_step3(2)
 
     for d in range(2):
         for r in range(2):
@@ -408,27 +436,32 @@
 
     def sent(u, carry):
         j, p = u % NC, u // NC
-        core_copy(j, p).wait_send()
+        @pl.when(c == 0)
+        def _():
+            core_copy(j, p).wait_send()
+
         for side in range(2):
             here = place(side)
 
-            @pl.when(here == NEAR)
+            @pl.when((c == 1) & (here == NEAR))
             def _():
                 near(j, p, side).wait_send()
 
-            @pl.when(here >= RELAY)
+            @pl.when((c == 1) & (here >= RELAY))
             def _():
                 chain(j, p, side).wait_send()
 
-            @pl.when(here == OWNER)
+            @pl.when((c == 1) & (here == OWNER))
             def _():
                 spread_near(j, p, side).wait_send()
 
-            @pl.when((here == OWNER) | (here == RELAY))
+            @pl.when((c == 1) & ((here == OWNER) | (here == RELAY)))
             def _():
                 spread(j, p, side).wait_send()
 
-            core_share(j, p, side).wait_send()
+            @pl.when(c == 1)
+            def _():
+                core_share(j, p, side).wait_send()
         return carry
 
     lax.fori_loop(0, 4 * NC, sent, 0)
@@ -453,10 +486,10 @@
             pltpu.VMEM((DM, FH), BF16),
             pltpu.VMEM((NC, 4, Q, DM), BF16),
             pltpu.VMEM((NC, 4, Q, DM), BF16),
-            pltpu.VMEM((NC, 4, 2, 2, 2, Q, GROUP), BF16),
-            pltpu.VMEM((NC, 4, 2, 2, Q, GROUP), BF16),
-            pltpu.VMEM((NC, 4, 2, 2, 2, Q, GROUP), BF16),
-            pltpu.VMEM((2, NC, 4, 4, Q, GROUP), BF16),
+            pltpu.VMEM((NC, 4, 2, 2, 2 * Q, GROUP), BF16),
+            pltpu.VMEM((NC, 4, 2, 2, 2 * Q, GROUP), BF16),
+            pltpu.VMEM((NC, 4, 2, 2, 2, 2 * Q, GROUP), BF16),
+            pltpu.VMEM((2, NC, 4, 2, 2 * Q, GROUP), BF16),
             pltpu.VMEM((NC, 2, 4, Q, DM), BF16),
             pltpu.VMEM((NC, 2, Q, DM), BF16),
             pltpu.VMEM((NC, 2, 2, Q, DM), BF16),

time: 109 us -> 89 us (0.82)
  Pallas kernels: 106 us -> 86 us
    pallas_call x1, Pallas kernels: 106 us -> 86 us  [per_device(): pl.pallas_call(kernel, out_shape=(jax.ShapeDtypeStruct((ROWS, DM), BF16),...]
where the time goes in v4:
time: 89 us; the launch traced here: 88.9 us
  Pallas kernels  86 us (97%)
  local copies, waits for them, and re-layouts  2.25 us (3%)
    pallas_call x1, Pallas kernels, per_device(): pl.pallas_call(kernel, out_shape=(jax.ShapeDtypeStruct((ROWS, DM), BF16),...  86 us
    unnamed x3, local copies, waits for them, and re-layouts  2.25 us

profile of v4, /device:TPU:1, one launch (start us, length us, event | category | flops | bytes accessed | tf_op | source)
XLA Modules:
  0.0 88.9 jit_solution(10663185651606222693)
XLA Ops:
  0.6 86.0 %mlp_branch.1 = (bf16[32,768]{1,0:T(8,128)(2,1)S(1)}, f32[192,768]{1,0:T(8,128)S(1)}, f32[192,768]{1,0:T(8,128)S(1)}) custom-call(bf16[32,768]{1,0:T(8,128)(2,1)} %normed.1, bf16[32,768]{1,0:T(8,128)(2,1)} %cotangent.1, bf16[768,768]{1,0:T(8,128)(2,1)} %w_in.1, bf16[4,3,64,768]{3,2,1,0:T(8,128)(2,1)} %bitcast.3), custom_call_target="tpu_custom_call" | custom-call | tf_op jit(solution)/shard_map/mlp_branch/pallas_call | solution.py:475
  86.6 0.6 copy.10
  87.3 0.8 copy.11
  88.1 0.8 copy.12

commit v5 on v4

--- a/solution.py
+++ b/solution.py
@@ -17,13 +17,13 @@
 FH = 768
 FC = FH // NC
 Q = FC // 4
-HALF = DM // 2
 
 K_OF_P = (0, 3, 1, 2)
 P_OF_K = (0, 2, 3, 1)
-STEP = (1, 3)
-
-UNITS = ((0, 0), (0, 1), (0, 2), (1, 0), (2, 0), (1, 1), (3, 0), (3, 1), (3, 2), (2, 1), (1, 2), (2, 2))
+STEP = (1, 3, 2)
+FROM = (3, 1, 2)
+
+UNITS = ((0, 0), (0, 1), (0, 2), (1, 0), (2, 0), (1, 1), (3, 0), (3, 1), (2, 1), (3, 2), (1, 2), (2, 2))
 GROUP_CODE = sum(p << (2 * n) for n, (p, j) in enumerate(UNITS))
 CHUNK_CODE = sum(j << (2 * n) for n, (p, j) in enumerate(UNITS))
 GROUP_FIRST = [min(n for n, u in enumerate(UNITS) if u[0] == p) for p in range(4)]
@@ -35,7 +35,7 @@
 S_BWD = S_FAR + 1
 STEPS = len(UNITS) + S_BWD
 X_STEP2 = 3
-Y_STEP2, Y_SUM = 2, 5
+Y_SUM = 4
 
 
 def nt(a, b):
@@ -61,10 +61,10 @@
 def kernel(
     normed, cotangent, w_in, w_out,
     ng_out, win_out, wout_out,
-    xg, win_v, w1t, wo, pu, crecv, zrecv, ah, dw, xr1, xr2, ngb, yr1, yr2, zs, gz1, gz2,
-    lsem, az_s, az_r, azf_s, azf_r, ay_s, ay_r, ayf_s, ayf_r,
+    xg, win_v, w1t, wo, pu, crecv, zrecv, ah, dw, xr1, xr2, ngb, yr, zs, zr,
+    lsem, az_s, az_r, azf_s, azf_r, ay_s, ay_r,
     co_s, co_r, ne_s, ne_r, ch_s, ch_r, sn_s, sn_r, sp_s, sp_r, ce_s, ce_r, x1_s, x1_r, x2_s, x2_r,
-    gy1_s, gy1_r, gy2_s, gy2_r, gz1_s, gz1_r, gz2_s, gz2_r,
+    gy_s, gy_r, gz_s, gz_r,
 ):
     x = lax.axis_index("dp")
     mx = lax.axis_index("mx")
@@ -98,7 +98,7 @@
         copy.start()
 
     barrier = pltpu.get_barrier_semaphore()
-    partners = [at_core]
+    partners = [at_core, at_y(2), at_zh(2)]
     for k in (1, 3):
         partners += [at_x(k), at_y(k), at_zh(k), at_zl(k)]
     for device in partners:
@@ -109,34 +109,26 @@
         return xg.at[a, p, yy, pl.ds(r * PIECE, PIECE)]
 
     def az(d, a, r):
-        there = rows(a, P_OF_K[STEP[1 - d]], 0, r)
+        there = rows(a, P_OF_K[FROM[d]], 0, r)
         return rc(rows(a, 0, 0, r), there, az_s.at[d, a, r], az_r.at[d, a, r], at_zh(STEP[d]))
 
     def azf(d, r):
-        here = rows(d, P_OF_K[STEP[1 - d]], 0, r)
+        here = rows(d, P_OF_K[FROM[d]], 0, r)
         return rc(here, rows(d, 3, 0, r), azf_s.at[d, r], azf_r.at[d, r], at_zh(STEP[d]))
 
     def ay(p, d, a, r):
-        there = rows(a, p, STEP[1 - d], r)
+        there = rows(a, p, FROM[d], r)
         return rc(rows(a, p, 0, r), there, ay_s.at[p, d, a, r], ay_r.at[p, d, a, r], at_y(STEP[d]))
 
-    def ayf(p, d, r):
-        here = rows(d, p, STEP[1 - d], r)
-        return rc(here, rows(d, p, 2, r), ayf_s.at[p, d, r], ayf_r.at[p, d, r], at_y(STEP[d]))
-
     def along_y(p, a, r):
-        for d in range(2):
+        for d in (2, 0, 1):
             ay(p, d, a, r).start()
 
-    def further_y(p, a, r):
-        ay(p, a, a, r).wait_recv()
-        ayf(p, a, r).start()
-
     def group_here(p):
-        for d in range(2):
-            for r in range(2):
-                ay(p, d, 1 - d, r).wait_recv()
-                ayf(p, d, r).wait_recv()
+        for d in range(3):
+            for a in range(2):
+                for r in range(2):
+                    ay(p, d, a, r).wait_recv()
 
     for copy in load_own:
         copy.wait()
@@ -144,8 +136,9 @@
         for r in range(2):
             az(0, a, r).start()
             az(1, 1 - a, r).start()
-            ay(0, 0, a, r).start()
-            ay(0, 1, 1 - a, r).start()
+    for a in range(2):
+        for r in range(2):
+            along_y(0, a, r)
 
     load_in.wait()
     for k in range(FH // 128):
@@ -164,34 +157,17 @@
                 az(d, a, r).wait_recv()
                 if d == a:
                     azf(d, r).start()
-                along_y(P_OF_K[STEP[1 - d]], a, r)
+                along_y(P_OF_K[FROM[d]], a, r)
         else:
             for d in range(2):
                 azf(d, w - 4).wait_recv()
                 along_y(3, d, w - 4)
 
-    def wave_on(w):
-        if w < 4:
-            for d, a, r in WAVES[w]:
-                further_y(P_OF_K[STEP[1 - d]], a, r)
-        else:
-            for d in range(2):
-                further_y(3, d, w - 4)
-
-    for r in range(2):
-        for a in range(2):
-            further_y(0, a, r)
     wave(0)
     wave(1)
+    group_here(0)
     wave(2)
-    wave_on(0)
-    group_here(0)
     wave(3)
-    wave_on(1)
-    wave(4)
-    wave_on(2)
-    wave(5)
-    wave_on(3)
 
     NEAR, OWNER, RELAY, FAR = range(4)
 
@@ -227,17 +203,11 @@
     def x2(j, d):
         return rc(dw.at[j, :, (x + STEP[d]) % 4], xr2.at[j, d], x2_s.at[j, d], x2_r.at[j, d], at_x(STEP[d]))
 
-    def y1(p, d):
-        return rc(ngb.at[p, 2, d], yr1.at[p, d], gy1_s.at[p, d], gy1_r.at[p, d], at_y(STEP[d]))
-
-    def y2(p, d):
-        return rc(ngb.at[p, STEP[d]], yr2.at[p, d], gy2_s.at[p, d], gy2_r.at[p, d], at_y(STEP[d]))
-
-    def z1(d):
-        return rc(zs.at[3, d], gz1.at[d], gz1_s.at[d], gz1_r.at[d], at_zh(STEP[d]))
-
-    def z2(d):
-        return rc(zs.at[P_OF_K[STEP[d]]], gz2.at[d], gz2_s.at[d], gz2_r.at[d], at_zh(STEP[d]))
+    def along_gy(p, d):
+        return rc(ngb.at[p, STEP[d]], yr.at[p, d], gy_s.at[p, d], gy_r.at[p, d], at_y(STEP[d]))
+
+    def along_gz(d):
+        return rc(zs.at[P_OF_K[STEP[d]]], zr.at[d], gz_s.at[d], gz_r.at[d], at_zh(STEP[d]))
 
     def forward(j, p):
         for a, w in enumerate((w1t, wo)):
@@ -300,10 +270,9 @@
 
     def normed_grad(j, p):
         total = tn(ah[1, :, p].reshape(FH, GROUP), w1t[...].reshape(FH, DM)).astype(BF16)
-        for h in range(2):
-            ngb[p, :, h] = total[:, h * HALF:(h + 1) * HALF].reshape(4, ROWS, HALF)
-        for d in range(2):
-            y1(p, d).start()
+        ngb[p] = total.reshape(4, ROWS, DM)
+        for d in (2, 0, 1):
+            along_gy(p, d).start()
 
     def x_step2(j):
         for d in range(2):
@@ -318,18 +287,17 @@
         for a, out in enumerate((win_out, wout_out)):
             out[j * Q:(j + 1) * Q] = dw[j, a, x].astype(F32) + xr2[j, 0, a].astype(F32) + xr2[j, 1, a].astype(F32)
 
-    def along_y2(p):
-        for d in range(2):
-            y1(p, d).wait_recv()
-            ngb[p, STEP[d], d] = (ngb[p, STEP[d], d].astype(F32) + yr1[p, d].astype(F32)).astype(BF16)
-            y2(p, d).start()
-
     def sum_y(p):
-        for d in range(2):
-            y2(p, d).wait_recv()
-        zs[p] = (ngb[p, 0].astype(F32) + yr2[p, 0].astype(F32) + yr2[p, 1].astype(F32)).astype(BF16)
-
-    AFTER = {1: lambda: wave_on(4), 2: lambda: wave_on(5)}
+        total = ngb[p, 0].astype(F32)
+        for d in range(3):
+            along_gy(p, d).wait_recv()
+            total = total + yr[p, d].astype(F32)
+        zs[p] = total.astype(BF16)
+        for d in range(3):
+            if P_OF_K[STEP[d]] == p:
+                along_gz(d).start()
+
+    AHEAD = {1: lambda: wave(4), 2: lambda: wave(5)}
 
     def step(tau, carry):
         def stage(s, run, on=None, core=None, among=None):
@@ -352,6 +320,8 @@
             def _():
                 run()
 
+        for n, run in AHEAD.items():
+            at(n, run)
         for side in range(2):
             stage(S_FAR, lambda j, p: take_far(j, p, side), (side, FAR))
             stage(S_BACK, lambda j, p: pass_back(j, p, side), (side, RELAY))
@@ -361,8 +331,6 @@
         for side in range(2):
             stage(S_RELAY, lambda j, p: pass_on(j, p, side), (side, RELAY))
         stage(S_ADD, add_core, core=1)
-        for n, run in AFTER.items():
-            at(n, run)
         for p in range(1, 4):
             at(GROUP_FIRST[p], lambda: group_here(p))
         stage(0, forward)
@@ -372,7 +340,6 @@
         for j in range(NC):
             at(CHUNK_LAST[j] + S_BWD + X_STEP2, lambda: x_step2(j))
         for p in range(4):
-            at(GROUP_LAST[p] + S_BWD + Y_STEP2, lambda: along_y2(p))
             at(GROUP_LAST[p] + S_BWD + Y_SUM, lambda: sum_y(p))
         return carry
 
@@ -382,57 +349,41 @@
         if CHUNK_LAST[j] + S_BWD + X_STEP2 >= STEPS:
             x_step2(j)
 
-    def rest_y2(p):
-        if GROUP_LAST[p] + S_BWD + Y_STEP2 >= STEPS:
-            along_y2(p)
-
     def rest_y(p):
         if GROUP_LAST[p] + S_BWD + Y_SUM >= STEPS:
             sum_y(p)
 
-    rest_y2(3)
     rest_y(0)
+    rest_y(3)
     rest_x(0)
-    rest_y(3)
-    for d in range(2):
-        z1(d).start()
-    rest_y2(1)
-    rest_y2(2)
     rest_x(1)
+    rest_y(1)
+    rest_y(2)
+    rest_x(2)
     x_step3(0)
-    rest_y(1)
-    rest_x(2)
-    rest_y(2)
-    for d in range(2):
-        z1(d).wait_recv()
-        p = P_OF_K[STEP[d]]
-        zs[p, d] = (zs[p, d].astype(F32) + gz1[d].astype(F32)).astype(BF16)
-        z2(d).start()
     x_step3(1)
-    for d in range(2):
-        z2(d).wait_recv()
-    total = zs[0].astype(F32) + gz2[0].astype(F32) + gz2[1].astype(F32)
-    for h in range(2):
-        ng_out[:, h * HALF:(h + 1) * HALF] = total[h].astype(BF16)
+    total = zs[0].astype(F32)
+    for d in (2, 0, 1):
+        along_gz(d).wait_recv()
+        total = total + zr[d].astype(F32)
+    ng_out[...] = total.astype(BF16)
     x_step3(2)
 
+    for d in range(3):
+        for p in range(4):
+            for a in range(2):
+                for r in range(2):
+                    ay(p, d, a, r).wait_send()
+            along_gy(p, d).wait_send()
+        along_gz(d).wait_send()
     for d in range(2):
         for r in range(2):
             for a in range(2):
                 az(d, a, r).wait_send()
             azf(d, r).wait_send()
-            for p in range(4):
-                for a in range(2):
-                    ay(p, d, a, r).wait_send()
-                ayf(p, d, r).wait_send()
-        for p in range(4):
-            y1(p, d).wait_send()
-            y2(p, d).wait_send()
         for j in range(NC):
             x1(j, d).wait_send()
             x2(j, d).wait_send()
-        z1(d).wait_send()
-        z2(d).wait_send()
 
     def sent(u, carry):
         j, p = u % NC, u // NC
@@ -493,17 +444,15 @@
             pltpu.VMEM((NC, 2, 4, Q, DM), BF16),
             pltpu.VMEM((NC, 2, Q, DM), BF16),
             pltpu.VMEM((NC, 2, 2, Q, DM), BF16),
-            pltpu.VMEM((4, 4, 2, ROWS, HALF), BF16),
-            pltpu.VMEM((4, 2, ROWS, HALF), BF16),
-            pltpu.VMEM((4, 2, 2, ROWS, HALF), BF16),
-            pltpu.VMEM((4, 2, ROWS, HALF), BF16),
-            pltpu.VMEM((2, ROWS, HALF), BF16),
-            pltpu.VMEM((2, 2, ROWS, HALF), BF16),
+            pltpu.VMEM((4, 4, ROWS, DM), BF16),
+            pltpu.VMEM((4, 3, ROWS, DM), BF16),
+            pltpu.VMEM((4, ROWS, DM), BF16),
+            pltpu.VMEM((3, ROWS, DM), BF16),
             pltpu.SemaphoreType.DMA((7,)),
-            *two(2, 2, 2), *two(2, 2), *two(4, 2, 2, 2), *two(4, 2, 2),
+            *two(2, 2, 2), *two(2, 2), *two(4, 3, 2, 2),
             *two(NC, 4), *two(NC, 4, 2), *two(NC, 4, 2), *two(NC, 4, 2), *two(NC, 4, 2), *two(NC, 4, 2),
             *two(NC, 2), *two(NC, 2),
-            *two(4, 2), *two(4, 2), *two(2), *two(2),
+            *two(4, 3), *two(3),
         ],
         compiler_params=pltpu.CompilerParams(
             collective_id=0, has_side_effects=True, vmem_limit_bytes=48 * 1024 * 1024

time: 89 us -> 86.9 us (0.976)
  Pallas kernels: 86 us -> 83.9 us
    pallas_call x1, Pallas kernels: 86 us -> 83.9 us  [per_device(): pl.pallas_call(kernel, out_shape=(jax.ShapeDtypeStruct((ROWS, DM), BF16),...]
where the time goes in v5:
time: 86.9 us; the launch traced here: 86.7 us
  Pallas kernels  83.9 us (97%)
  local copies, waits for them, and re-layouts  2.25 us (3%)
    pallas_call x1, Pallas kernels, per_device(): pl.pallas_call(kernel, out_shape=(jax.ShapeDtypeStruct((ROWS, DM), BF16),...  83.9 us
    unnamed x3, local copies, waits for them, and re-layouts  2.25 us

profile of v5, /device:TPU:1, one launch (start us, length us, event | category | flops | bytes accessed | tf_op | source)
XLA Modules:
  0.0 86.7 jit_solution(7767794689807613087)
XLA Ops:
  0.6 83.9 %mlp_branch.1 = (bf16[32,768]{1,0:T(8,128)(2,1)S(1)}, f32[192,768]{1,0:T(8,128)S(1)}, f32[192,768]{1,0:T(8,128)S(1)}) custom-call(bf16[32,768]{1,0:T(8,128)(2,1)} %normed.1, bf16[32,768]{1,0:T(8,128)(2,1)} %cotangent.1, bf16[768,768]{1,0:T(8,128)(2,1)} %w_in.1, bf16[4,3,64,768]{3,2,1,0:T(8,128)(2,1)} %bitcast.3), custom_call_target="tpu_custom_call" | custom-call | tf_op jit(solution)/shard_map/mlp_branch/pallas_call | solution.py:426
  84.5 0.6 copy.10
  85.1 0.8 copy.11
  85.9 0.8 copy.12

commit v6 on v5

--- a/solution.py
+++ b/solution.py
@@ -60,9 +60,9 @@
 
 def kernel(
     normed, cotangent, w_in, w_out,
-    ng_out, win_out, wout_out,
+    ng_out, grads_out,
     xg, win_v, w1t, wo, pu, crecv, zrecv, ah, dw, xr1, xr2, ngb, yr, zs, zr,
-    lsem, az_s, az_r, azf_s, azf_r, ay_s, ay_r,
+    lsem, az_s, az_r, azf_s, azf_r, ay_s, ay_r, ayf_s, ayf_r,
     co_s, co_r, ne_s, ne_r, ch_s, ch_r, sn_s, sn_r, sp_s, sp_r, ce_s, ce_r, x1_s, x1_r, x2_s, x2_r,
     gy_s, gy_r, gz_s, gz_r,
 ):
@@ -120,15 +120,22 @@
         there = rows(a, p, FROM[d], r)
         return rc(rows(a, p, 0, r), there, ay_s.at[p, d, a, r], ay_r.at[p, d, a, r], at_y(STEP[d]))
 
+    def ayf(d, r):
+        return rc(rows(d, 0, FROM[d], r), rows(d, 0, 2, r), ayf_s.at[d, r], ayf_r.at[d, r], at_y(STEP[d]))
+
     def along_y(p, a, r):
-        for d in (2, 0, 1):
+        for d in (2, 0, 1) if p > 0 else (a, 1 - a):
             ay(p, d, a, r).start()
 
     def group_here(p):
-        for d in range(3):
-            for a in range(2):
-                for r in range(2):
-                    ay(p, d, a, r).wait_recv()
+        for a in range(2):
+            for r in range(2):
+                ay(p, 1 - a, a, r).wait_recv()
+                if p > 0:
+                    ay(p, a, a, r).wait_recv()
+                    ay(p, 2, a, r).wait_recv()
+                else:
+                    ayf(a, r).wait_recv()
 
     for copy in load_own:
         copy.wait()
@@ -163,11 +170,14 @@
                 azf(d, w - 4).wait_recv()
                 along_y(3, d, w - 4)
 
+    for r in range(2):
+        for a in range(2):
+            ay(0, a, a, r).wait_recv()
+            ayf(a, r).start()
     wave(0)
     wave(1)
     group_here(0)
     wave(2)
-    wave(3)
 
     NEAR, OWNER, RELAY, FAR = range(4)
 
@@ -284,8 +294,10 @@
     def x_step3(j):
         for d in range(2):
             x2(j, d).wait_recv()
-        for a, out in enumerate((win_out, wout_out)):
-            out[j * Q:(j + 1) * Q] = dw[j, a, x].astype(F32) + xr2[j, 0, a].astype(F32) + xr2[j, 1, a].astype(F32)
+        for a in range(2):
+            grads_out[a, j * Q:(j + 1) * Q] = (
+                dw[j, a, x].astype(F32) + xr2[j, 0, a].astype(F32) + xr2[j, 1, a].astype(F32)
+            )
 
     def sum_y(p):
         total = ngb[p, 0].astype(F32)
@@ -297,7 +309,7 @@
             if P_OF_K[STEP[d]] == p:
                 along_gz(d).start()
 
-    AHEAD = {1: lambda: wave(4), 2: lambda: wave(5)}
+    AHEAD = {0: lambda: wave(3), 1: lambda: wave(4), 2: lambda: wave(5)}
 
     def step(tau, carry):
         def stage(s, run, on=None, core=None, among=None):
@@ -358,8 +370,8 @@
     rest_x(0)
     rest_x(1)
     rest_y(1)
+    rest_x(2)
     rest_y(2)
-    rest_x(2)
     x_step3(0)
     x_step3(1)
     total = zs[0].astype(F32)
@@ -373,7 +385,8 @@
         for p in range(4):
             for a in range(2):
                 for r in range(2):
-                    ay(p, d, a, r).wait_send()
+                    if d < 2 or p > 0:
+                        ay(p, d, a, r).wait_send()
             along_gy(p, d).wait_send()
         along_gz(d).wait_send()
     for d in range(2):
@@ -381,6 +394,7 @@
             for a in range(2):
                 az(d, a, r).wait_send()
             azf(d, r).wait_send()
+            ayf(d, r).wait_send()
         for j in range(NC):
             x1(j, d).wait_send()
             x2(j, d).wait_send()
@@ -423,15 +437,14 @@
     hbm = pl.BlockSpec(memory_space=pltpu.HBM)
     two = lambda *shape: [pltpu.SemaphoreType.DMA(shape)] * 2
     inputs = (normed, cotangent, w_in, w_out.reshape(4, NC, Q, DM))
-    ng, win_t, wout = pl.pallas_call(
+    ng, grads = pl.pallas_call(
         kernel,
         out_shape=(
             jax.ShapeDtypeStruct((ROWS, DM), BF16),
-            jax.ShapeDtypeStruct((FH // 4, DM), F32),
-            jax.ShapeDtypeStruct((FH // 4, DM), F32),
+            jax.ShapeDtypeStruct((2, FH // 4, DM), F32),
         ),
         in_specs=[hbm, hbm, hbm, hbm],
-        out_specs=[vmem, vmem, vmem],
+        out_specs=[vmem, vmem],
         scratch_shapes=[
             pltpu.VMEM((2, 4, 4, ROWS, DM), BF16),
             pltpu.VMEM((DM, FH), BF16),
@@ -449,7 +462,7 @@
             pltpu.VMEM((4, ROWS, DM), BF16),
             pltpu.VMEM((3, ROWS, DM), BF16),
             pltpu.SemaphoreType.DMA((7,)),
-            *two(2, 2, 2), *two(2, 2), *two(4, 3, 2, 2),
+            *two(2, 2, 2), *two(2, 2), *two(4, 3, 2, 2), *two(2, 2),
             *two(NC, 4), *two(NC, 4, 2), *two(NC, 4, 2), *two(NC, 4, 2), *two(NC, 4, 2), *two(NC, 4, 2),
             *two(NC, 2), *two(NC, 2),
             *two(4, 3), *two(3),
@@ -459,7 +472,7 @@
         ),
         name="mlp_branch",
     )(*[pltpu.with_memory_space_constraint(t, pltpu.HBM) for t in inputs])
-    return ng, win_t.T, wout
+    return ng, grads[0].T, grads[1]
 
 
 def solution(mesh):

time: 86.9 us -> 86.4 us (level)
    unnamed x3 -> x1, local copies, waits for them, and re-layouts: 2.25 us -> 0.62 us
    squeeze x0 -> x1, local copies, waits for them, and re-layouts: none -> 1.09 us  [per_device(): return (ng, grads[0].T, grads[1])]
where the time goes in v6:
time: 86.4 us; the launch traced here: 86.3 us
  Pallas kernels  83.9 us (97%)
  local copies, waits for them, and re-layouts  1.71 us (2%)
    pallas_call x1, Pallas kernels, per_device(): pl.pallas_call(kernel, out_shape=(jax.ShapeDtypeStruct((ROWS, DM), BF16),...  83.9 us

profile of v6, /device:TPU:1, one launch (start us, length us, event | category | flops | bytes accessed | tf_op | source)
XLA Modules:
  0.0 86.3 jit_solution(6914253029245564968)
XLA Ops:
  0.6 83.9 %mlp_branch.1 = (bf16[32,768]{1,0:T(8,128)(2,1)S(1)}, f32[2,192,768]{2,1,0:T(8,128)S(1)}) custom-call(bf16[32,768]{1,0:T(8,128)(2,1)} %normed.1, bf16[32,768]{1,0:T(8,128)(2,1)} %cotangent.1, bf16[768,768]{1,0:T(8,128)(2,1)} %w_in.1, bf16[4,3,64,768]{3,2,1,0:T(8,128)(2,1)} %bitcast.7), custom_call_target="tpu_custom_call" | custom-call | tf_op jit(solution)/shard_map/mlp_branch/pallas_call | solution.py:440
  84.6 1.1 %slice_bitcast_fusion = (f32[192,768]{1,0:T(8,128)}, f32[768,192]{0,1:T(8,128)}) fusion(f32[2,192,768]{2,1,0:T(8,128)S(1)} %get-tuple-element.6), kind=kLoop, calls=%fused_computation | loop fusion | bytes 2359296 | tf_op jit(solution)/shard_map/squeeze | solution.py:475
  85.6 0.6 copy.8

commit v7 on v6

--- a/solution.py
+++ b/solution.py
@@ -372,6 +372,51 @@
     rest_y(1)
     rest_x(2)
     rest_y(2)
+    for d in range(3):
+        for p in range(4):
+            for a in range(2):
+                for r in range(2):
+                    if d < 2 or p > 0:
+                        ay(p, d, a, r).wait_send()
+    for d in range(2):
+        for r in range(2):
+            for a in range(2):
+                az(d, a, r).wait_send()
+            azf(d, r).wait_send()
+            ayf(d, r).wait_send()
+
+    def sent(u, carry):
+        j, p = u % NC, u // NC
+        @pl.when(c == 0)
+        def _():
+            core_copy(j, p).wait_send()
+
+        for side in range(2):
+            here = place(side)
+
+            @pl.when((c == 1) & (here == NEAR))
+            def _():
+                near(j, p, side).wait_send()
+
+            @pl.when((c == 1) & (here >= RELAY))
+            def _():
+                chain(j, p, side).wait_send()
+
+            @pl.when((c == 1) & (here == OWNER))
+            def _():
+                spread_near(j, p, side).wait_send()
+
+            @pl.when((c == 1) & ((here == OWNER) | (here == RELAY)))
+            def _():
+                spread(j, p, side).wait_send()
+
+            @pl.when(c == 1)
+            def _():
+                core_share(j, p, side).wait_send()
+        return carry
+
+    lax.fori_loop(0, 4 * NC, sent, 0)
+
     x_step3(0)
     x_step3(1)
     total = zs[0].astype(F32)
@@ -383,53 +428,12 @@
 
     for d in range(3):
         for p in range(4):
-            for a in range(2):
-                for r in range(2):
-                    if d < 2 or p > 0:
-                        ay(p, d, a, r).wait_send()
             along_gy(p, d).wait_send()
         along_gz(d).wait_send()
     for d in range(2):
-        for r in range(2):
-            for a in range(2):
-                az(d, a, r).wait_send()
-            azf(d, r).wait_send()
-            ayf(d, r).wait_send()
         for j in range(NC):
             x1(j, d).wait_send()
             x2(j, d).wait_send()
-
-    def sent(u, carry):
-        j, p = u % NC, u // NC
-        @pl.when(c == 0)
-        def _():
-            core_copy(j, p).wait_send()
-
-        for side in range(2):
-            here = place(side)
-
-            @pl.when((c == 1) & (here == NEAR))
-            def _():
-                near(j, p, side).wait_send()
-
-            @pl.when((c == 1) & (here >= RELAY))
-            def _():
-                chain(j, p, side).wait_send()
-
-            @pl.when((c == 1) & (here == OWNER))
-            def _():
-                spread_near(j, p, side).wait_send()
-
-            @pl.when((c == 1) & ((here == OWNER) | (here == RELAY)))
-            def _():
-                spread(j, p, side).wait_send()
-
-            @pl.when(c == 1)
-            def _():
-                core_share(j, p, side).wait_send()
-        return carry
-
-    lax.fori_loop(0, 4 * NC, sent, 0)
 
 
 def per_device(normed, cotangent, w_in, w_out):

time: 86.4 us -> 85.9 us (level)
  no operation moved by 1% of the time
where the time goes in v7:
time: 85.9 us; the launch traced here: 85.8 us
  Pallas kernels  83.4 us (97%)
  local copies, waits for them, and re-layouts  1.71 us (2%)
    pallas_call x1, Pallas kernels, per_device(): pl.pallas_call(kernel, out_shape=(jax.ShapeDtypeStruct((ROWS, DM), BF16),...  83.4 us

profile of v7, /device:TPU:1, one launch (start us, length us, event | category | flops | bytes accessed | tf_op | source)
XLA Modules:
  0.0 85.8 jit_solution(4270396446164326068)
XLA Ops:
  0.6 83.4 %mlp_branch.1 = (bf16[32,768]{1,0:T(8,128)(2,1)S(1)}, f32[2,192,768]{2,1,0:T(8,128)S(1)}) custom-call(bf16[32,768]{1,0:T(8,128)(2,1)} %normed.1, bf16[32,768]{1,0:T(8,128)(2,1)} %cotangent.1, bf16[768,768]{1,0:T(8,128)(2,1)} %w_in.1, bf16[4,3,64,768]{3,2,1,0:T(8,128)(2,1)} %bitcast.7), custom_call_target="tpu_custom_call" | custom-call | tf_op jit(solution)/shard_map/mlp_branch/pallas_call | solution.py:444
  84.1 1.1 %slice_bitcast_fusion = (f32[192,768]{1,0:T(8,128)}, f32[768,192]{0,1:T(8,128)}) fusion(f32[2,192,768]{2,1,0:T(8,128)S(1)} %get-tuple-element.6), kind=kLoop, calls=%fused_computation | loop fusion | bytes 2359296 | tf_op jit(solution)/shard_map/squeeze | solution.py:479
  85.2 0.6 copy.8
